TPU v7x, 32 devices: a whole 2x2x4 slice. The times are simulated.
32 devices in a mesh: fsdp: 4 (over y, x), ctx: 4 (over z), tp: 2 (over core).
Axes of the slice: x: 2, y: 2, z: 4, core: 2. Of those that a mesh axis runs over, the one named last changes fastest.
Arguments:
- tokens: bfloat16 [4096, 1024], P(('fsdp', 'ctx'), 'tp'), may hold values from -6 to 6
- w_query: bfloat16 [1024, 1024], P('fsdp', 'tp'), may hold values from -0.1875 to 0.1875
- w_key: bfloat16 [1024, 1024], P('fsdp', 'tp'), may hold values from -0.1875 to 0.1875
- w_value: bfloat16 [1024, 1024], P('fsdp', 'tp'), may hold values from -0.1875 to 0.1875
- w_attn_out: bfloat16 [1024, 1024], P('tp', 'fsdp'), may hold values from -2.5 to 2.5
- w_in: bfloat16 [1024, 4096], P('fsdp', 'tp'), may hold values from -0.1875 to 0.1875
- w_down: bfloat16 [4096, 1024], P('tp', 'fsdp'), may hold values from -0.09375 to 0.09375
- vectors: bfloat16 [8, 1024], P(None, 'tp'), may hold values from -0.4 to 1.4
- bias_in: bfloat16 [4096], P('tp'), may hold values from -0.59765625 to 0.59765625
- lengths: int32 [4], P('fsdp'), may hold values from 256 to 1024, as said below
- cotangent: bfloat16 [4096, 1024], P(('fsdp', 'ctx'), 'tp'), may hold values from -6 to 6
Outputs:
- output: bfloat16 [4096, 1024], P(('fsdp', 'ctx'), 'tp')
- grad_tokens: float32 [4096, 1024], P(('fsdp', 'ctx'), 'tp')
- grad_query: float32 [1024, 1024], P('fsdp', 'tp')
- grad_key: float32 [1024, 1024], P('fsdp', 'tp')
- grad_value: float32 [1024, 1024], P('fsdp', 'tp')
- grad_attn_out: float32 [1024, 1024], P('tp', 'fsdp')
- grad_in: float32 [1024, 4096], P('fsdp', 'tp')
- grad_down: float32 [4096, 1024], P('tp', 'fsdp')
- grad_vectors: float32 [8, 1024], P(None, ('tp', 'fsdp'))
- grad_bias_in: float32 [4096], P(('tp', 'fsdp'))
Inputs may be any that keep to these rules, and one draw needn't show every extreme that they name: `lengths`: real positions fill the first slots of a sequence; at least one sequence has 1024.
All inputs are finite; a program needn't handle non-finite values.
Results may differ from a plain program's by a relative error of at most 0.02.
Values may be sent and summed in bfloat16 or wider, within the bound.
A program may use at most 128 MiB of HBM per device.

v0:
```python
import jax
import jax.numpy as jnp
from jax import lax
from jax.sharding import PartitionSpec as P

HEAD = 64


norm_eps = 1e-06
masked_score = -1e30


def matmul_plain(left_side, right_side):
    return jnp.dot(left_side, right_side, preferred_element_type=jnp.float32)


def matmul_left_t(left_side, right_side):
    return lax.dot_general(
        left_side, right_side, (((0,), (0,)), ((), ())), preferred_element_type=jnp.float32
    )


def matmul_right_t(left_side, right_side):
    return lax.dot_general(
        left_side, right_side, (((1,), (1,)), ((), ())), preferred_element_type=jnp.float32
    )


def norm_forward(values_in, gain_row, shift_row):
    center = values_in - jnp.mean(values_in, axis=-1, keepdims=True)
    spread = jnp.mean(center * center, axis=-1, keepdims=True)
    inv_dev = lax.rsqrt(spread + norm_eps)
    normed = center * inv_dev
    return (normed * gain_row + shift_row, normed, inv_dev)


def norm_backward(grad_out, gain_row, normed, inv_dev):
    grad_normed = grad_out * gain_row
    mean_plain = jnp.mean(grad_normed, axis=-1, keepdims=True)
    mean_normed = jnp.mean(grad_normed * normed, axis=-1, keepdims=True)
    return inv_dev * (grad_normed - mean_plain - normed * mean_normed)


def gelu_exact(values_in):
    return jax.nn.gelu(values_in, approximate=False)


def tensor_total(partial_rows):
    return lax.psum(partial_rows, "tp")


def pick_pair(matrix, block_index, pair_width):
    columns = lax.dynamic_slice_in_dim(matrix, block_index * pair_width, pair_width, 1)
    return columns.reshape(matrix.shape[0], 2, pair_width // 2)


def own_columns(matrix, tp_rank, half_width):
    return lax.dynamic_slice_in_dim(matrix, tp_rank * half_width, half_width, matrix.ndim - 1)


def join_blocks(blocks, half_width):
    return blocks.transpose(1, 0, 2).reshape(blocks.shape[1], half_width)


def per_device(
    tokens, w_query, w_key, w_value, w_attn_out, w_in, w_down, vectors, bias_in, lengths, cotangent
):
    row_count, half_width = tokens.shape
    tp_rank = lax.axis_index("tp")
    ctx_rank = lax.axis_index("ctx")
    seq_slots = row_count * lax.axis_size("ctx")
    pair_width = 2 * HEAD
    block_count = half_width // pair_width
    tok_full, cot_full, vec_full = (
        lax.all_gather(tokens, "tp", axis=1, tiled=True),
        lax.all_gather(cotangent, "tp", axis=1, tiled=True),
        lax.all_gather(vectors, "tp", axis=1, tiled=True),
    )
    w_q, w_k, w_v, w_o, w_i, w_d = (
        lax.all_gather(w_query, "fsdp", axis=0, tiled=True),
        lax.all_gather(w_key, "fsdp", axis=0, tiled=True),
        lax.all_gather(w_value, "fsdp", axis=0, tiled=True),
        lax.all_gather(w_attn_out, "fsdp", axis=1, tiled=True),
        lax.all_gather(w_in, "fsdp", axis=0, tiled=True),
        lax.all_gather(w_down, "fsdp", axis=1, tiled=True),
    )
    vec_rows = vec_full.astype(jnp.float32)
    own_vec = vectors.astype(jnp.float32)
    seq_length = lengths[0]
    key_valid = jnp.arange(seq_slots) < seq_length
    row_valid = ctx_rank * row_count + jnp.arange(row_count) < seq_length
    seed_grad = cot_full.astype(jnp.float32) * row_valid[:, None].astype(jnp.float32)
    tok_float = tok_full.astype(jnp.float32)
    queries = ((matmul_plain(tok_full, w_q) + own_vec[0]) * 0.125).astype(jnp.bfloat16)
    keys_own = matmul_plain(tok_full, w_k).astype(jnp.bfloat16)
    values_own = (matmul_plain(tok_full, w_v) + own_vec[1]).astype(jnp.bfloat16)
    keys_all, values_all = (
        lax.all_gather(keys_own, "ctx", axis=0, tiled=True),
        lax.all_gather(values_own, "ctx", axis=0, tiled=True),
    )

    def block_scores(block_index):
        head_q = pick_pair(queries, block_index, pair_width)
        head_k = pick_pair(keys_all, block_index, pair_width)
        scores = jnp.einsum("qhd,khd->hqk", head_q, head_k, preferred_element_type=jnp.float32)
        return (jnp.where(key_valid[None, None, :], scores, masked_score), head_q, head_k)

    def attend_block(block_index):
        scores, head_q, head_k = block_scores(block_index)
        head_v = pick_pair(values_all, block_index, pair_width)
        top_score = jnp.max(scores, axis=-1, keepdims=True)
        weights_exp = jnp.exp(scores - top_score)
        total = jnp.sum(weights_exp, axis=-1, keepdims=True)
        probs_low = (weights_exp / total).astype(jnp.bfloat16)
        mixed = jnp.einsum("hqk,khd->qhd", probs_low, head_v, preferred_element_type=jnp.float32)
        return (mixed.reshape(row_count, pair_width), top_score + jnp.log(total))

    mixed_blocks, log_totals = lax.map(attend_block, jnp.arange(block_count))
    context = join_blocks(mixed_blocks, half_width).astype(jnp.bfloat16)
    attended = tensor_total(matmul_plain(context, w_o))
    hidden_one, normed_one, inv_one = norm_forward(
        tok_float + attended + vec_rows[2], vec_rows[4], vec_rows[5]
    )
    hidden_low = hidden_one.astype(jnp.bfloat16)
    pre_act = matmul_plain(hidden_low, w_i) + bias_in.astype(jnp.float32)
    activated, gelu_pull = jax.vjp(gelu_exact, pre_act)
    act_low = activated.astype(jnp.bfloat16)
    branch = tensor_total(matmul_plain(act_low, w_d))
    layer_out, normed_two, inv_two = norm_forward(
        hidden_one + branch + vec_rows[3], vec_rows[6], vec_rows[7]
    )
    output_rows = own_columns(layer_out, tp_rank, half_width).astype(jnp.bfloat16)
    grad_two = norm_backward(seed_grad, vec_rows[6], normed_two, inv_two)
    branch_low = grad_two.astype(jnp.bfloat16)
    grad_down = matmul_left_t(act_low, branch_low)
    grad_pre = gelu_pull(matmul_right_t(branch_low, w_d))[0]
    pre_low = grad_pre.astype(jnp.bfloat16)
    grad_up = matmul_left_t(hidden_low, pre_low)
    grad_hidden = grad_two + tensor_total(matmul_right_t(pre_low, w_i))
    grad_one = norm_backward(grad_hidden, vec_rows[4], normed_one, inv_one)
    attn_low = grad_one.astype(jnp.bfloat16)
    grad_out_proj = matmul_left_t(context, attn_low)
    grad_context = matmul_right_t(attn_low, w_o).astype(jnp.bfloat16)

    def attend_back(pair_args):
        block_index, log_total = pair_args
        scores, head_q, head_k = block_scores(block_index)
        head_v = pick_pair(values_all, block_index, pair_width)
        head_g = pick_pair(grad_context, block_index, pair_width)
        probs = jnp.exp(scores - log_total)
        grad_probs = jnp.einsum("qhd,khd->hqk", head_g, head_v, preferred_element_type=jnp.float32)
        inner = jnp.sum(probs * grad_probs, axis=-1, keepdims=True)
        grad_scores = (probs * (grad_probs - inner)).astype(jnp.bfloat16)
        grad_q = jnp.einsum("hqk,khd->qhd", grad_scores, head_k, preferred_element_type=jnp.float32)
        grad_k = jnp.einsum("hqk,qhd->khd", grad_scores, head_q, preferred_element_type=jnp.float32)
        grad_v = jnp.einsum(
            "hqk,qhd->khd", probs.astype(jnp.bfloat16), head_g, preferred_element_type=jnp.float32
        )
        return (
            grad_q.reshape(row_count, pair_width),
            grad_k.reshape(seq_slots, pair_width),
            grad_v.reshape(seq_slots, pair_width),
        )

    query_blocks, key_blocks, value_blocks = lax.map(
        attend_back, (jnp.arange(block_count), log_totals)
    )
    grad_keys, grad_values = (
        lax.psum_scatter(
            join_blocks(key_blocks, half_width).astype(jnp.bfloat16),
            "ctx",
            scatter_dimension=0,
            tiled=True,
        ).astype(jnp.float32),
        lax.psum_scatter(
            join_blocks(value_blocks, half_width).astype(jnp.bfloat16),
            "ctx",
            scatter_dimension=0,
            tiled=True,
        ).astype(jnp.float32),
    )
    query_low = join_blocks(query_blocks, half_width).astype(jnp.bfloat16) * 0.125
    key_low = grad_keys.astype(jnp.bfloat16)
    value_low = grad_values.astype(jnp.bfloat16)
    grad_wq = matmul_left_t(tok_full, query_low)
    grad_wk = matmul_left_t(tok_full, key_low)
    grad_wv = matmul_left_t(tok_full, value_low)
    input_part = (
        matmul_right_t(query_low, w_q)
        + matmul_right_t(key_low, w_k)
        + matmul_right_t(value_low, w_v)
    )
    grad_tokens = lax.psum_scatter(
        input_part.astype(jnp.bfloat16), "tp", scatter_dimension=1, tiled=True
    ).astype(jnp.float32) + own_columns(grad_one, tp_rank, half_width)
    vector_grads = jnp.stack(
        [
            jnp.sum(query_low.astype(jnp.float32), axis=0),
            jnp.sum(value_low.astype(jnp.float32), axis=0),
            own_columns(jnp.sum(grad_one, axis=0), tp_rank, half_width),
            own_columns(jnp.sum(grad_two, axis=0), tp_rank, half_width),
            own_columns(jnp.sum(grad_hidden * normed_one, axis=0), tp_rank, half_width),
            own_columns(jnp.sum(grad_hidden, axis=0), tp_rank, half_width),
            own_columns(jnp.sum(seed_grad * normed_two, axis=0), tp_rank, half_width),
            own_columns(jnp.sum(seed_grad, axis=0), tp_rank, half_width),
        ]
    )
    bias_grad = jnp.sum(pre_low.astype(jnp.float32), axis=0)
    grad_parts = (
        grad_wq,
        grad_wk,
        grad_wv,
        grad_out_proj,
        grad_up,
        grad_down,
        vector_grads,
        bias_grad,
    )
    summed = (
        lax.psum_scatter(
            grad_parts[0].astype(jnp.bfloat16), "fsdp", scatter_dimension=0, tiled=True
        ).astype(jnp.float32),
        lax.psum_scatter(
            grad_parts[1].astype(jnp.bfloat16), "fsdp", scatter_dimension=0, tiled=True
        ).astype(jnp.float32),
        lax.psum_scatter(
            grad_parts[2].astype(jnp.bfloat16), "fsdp", scatter_dimension=0, tiled=True
        ).astype(jnp.float32),
        lax.psum_scatter(
            grad_parts[3].astype(jnp.bfloat16), "fsdp", scatter_dimension=1, tiled=True
        ).astype(jnp.float32),
        lax.psum_scatter(
            grad_parts[4].astype(jnp.bfloat16), "fsdp", scatter_dimension=0, tiled=True
        ).astype(jnp.float32),
        lax.psum_scatter(
            grad_parts[5].astype(jnp.bfloat16), "fsdp", scatter_dimension=1, tiled=True
        ).astype(jnp.float32),
        lax.psum_scatter(
            grad_parts[6].astype(jnp.bfloat16), "fsdp", scatter_dimension=1, tiled=True
        ).astype(jnp.float32),
        lax.psum_scatter(
            grad_parts[7].astype(jnp.bfloat16), "fsdp", scatter_dimension=0, tiled=True
        ).astype(jnp.float32),
    )
    summed = (
        lax.psum(summed[0].astype(jnp.bfloat16), "ctx").astype(jnp.float32),
        lax.psum(summed[1].astype(jnp.bfloat16), "ctx").astype(jnp.float32),
        lax.psum(summed[2].astype(jnp.bfloat16), "ctx").astype(jnp.float32),
        lax.psum(summed[3].astype(jnp.bfloat16), "ctx").astype(jnp.float32),
        lax.psum(summed[4].astype(jnp.bfloat16), "ctx").astype(jnp.float32),
        lax.psum(summed[5].astype(jnp.bfloat16), "ctx").astype(jnp.float32),
        lax.psum(summed[6].astype(jnp.bfloat16), "ctx").astype(jnp.float32),
        lax.psum(summed[7].astype(jnp.bfloat16), "ctx").astype(jnp.float32),
    )
    return (
        output_rows,
        grad_tokens,
        summed[0],
        summed[1],
        summed[2],
        summed[3],
        summed[4],
        summed[5],
        summed[6],
        summed[7],
    )


def solution(mesh):
    placed = (
        P(("fsdp", "ctx"), "tp"),
        P("fsdp", "tp"),
        P("fsdp", "tp"),
        P("fsdp", "tp"),
        P("tp", "fsdp"),
        P("fsdp", "tp"),
        P("tp", "fsdp"),
        P(None, "tp"),
        P("tp"),
        P("fsdp"),
        P(("fsdp", "ctx"), "tp"),
    )
    return jax.shard_map(
        per_device,
        mesh=mesh,
        in_specs=placed,
        out_specs=(
            P(("fsdp", "ctx"), "tp"),
            P(("fsdp", "ctx"), "tp"),
            P("fsdp", "tp"),
            P("fsdp", "tp"),
            P("fsdp", "tp"),
            P("tp", "fsdp"),
            P("fsdp", "tp"),
            P("tp", "fsdp"),
            P(None, ("tp", "fsdp")),
            P(("tp", "fsdp")),
        ),
        check_vma=False,
    )
```

profile of v0, /device:TPU:9, one launch (start us, length us, event | category | flops | bytes accessed | tf_op | source)
XLA Modules:
  0.0 880.3 jit_solution(6318413549660934292)
XLA Ops:
  12.9 24.8 %all-gather.9.cloned.1.call-done = bf16[1024,512]{1,0:T(8,128)(2,1)} async-done(((bf16[256,512]{1,0:T(8,128)(2,1)}), bf16[1024,512]{1,0:T(8,128)(2,1)}) %all-gather.9.cloned.1.call-update) | async-done | bytes 1048592 | tf_op jit(solution)/shard_map/all_gather | solution.py:82
  40.1 26.1 %all-gather.15.cloned.1.call-done = bf16[1024,512]{1,0:T(8,128)(2,1)} async-done(((bf16[256,512]{1,0:T(8,128)(2,1)}), bf16[1024,512]{1,0:T(8,128)(2,1)}) %all-gather.15.cloned.1.call-update) | async-done | bytes 1048592 | tf_op jit(solution)/shard_map/all_gather | solution.py:81
  69.2 25.5 %all-gather.13.cloned.1.call-done = bf16[1024,512]{1,0:T(8,128)(2,1)} async-done(((bf16[256,512]{1,0:T(8,128)(2,1)}), bf16[1024,512]{1,0:T(8,128)(2,1)}) %all-gather.13.cloned.1.call-update) | async-done | bytes 1048592 | tf_op jit(solution)/shard_map/all_gather | solution.py:80
  96.5 27.9 %all-gather.11.cloned.1.call-done = bf16[1024,512]{1,0:T(8,128)(2,1)} async-done(((bf16[256,512]{1,0:T(8,128)(2,1)}), bf16[1024,512]{1,0:T(8,128)(2,1)}) %all-gather.11.cloned.1.call-update) | async-done | bytes 1048592 | tf_op jit(solution)/shard_map/all_gather | solution.py:99
  125.9 28.0 %all-gather.17.cloned.1.call-done = bf16[1024,512]{1,0:T(8,128)(2,1)} async-done(((bf16[256,512]{1,0:T(8,128)(2,1)}), bf16[1024,512]{1,0:T(8,128)(2,1)}) %all-gather.17.cloned.1.call-update) | async-done | bytes 1048592 | tf_op jit(solution)/shard_map/all_gather | solution.py:98
  155.4 15.1 %while.28 = (s32[]{:T(128)}, bf16[4,256,128]{1,2,0:T(8,128)(2,1)S(1)}, f32[4,2,256,1]{2,1,3,0:T(2,128)S(1)}, s32[4]{0:T(128)S(1)}, bf16[1024,512]{0,1:T(8,128)(2...) while((s32[]{:T(128)}, ...), condition=%wide.region_3.4_spmd.clone, body=%wide.region_0.3_spmd.clone.sunk | while | flops 138936832 | bytes 8278219 | solution.py:118
  170.5 11.3 %all-gather.19.cloned.1.call-done = bf16[512,1024]{1,0:T(8,128)(2,1)} async-done(((bf16[512,256]{1,0:T(8,128)(2,1)}), bf16[512,1024]{1,0:T(8,128)(2,1)}) %all-gather.19.cloned.1.call-update) | async-done | bytes 1048592 | tf_op jit(solution)/shard_map/all_gather | solution.py:83
  188.3 16.8 %all-reduce.8.cloned.1.call-done = f32[256,1024]{1,0:T(8,128)} async-done(((f32[256,1024]{1,0:T(8,128)}), f32[256,1024]{1,0:T(8,128)}) %all-reduce.8.cloned.1.call-update) | async-done | bytes 1048592 | tf_op jit(solution)/shard_map/psum | solution.py:49
  206.8 53.5 %all-gather.21.cloned.1.call-done = bf16[1024,2048]{1,0:T(8,128)(2,1)} async-done(((bf16[256,2048]{1,0:T(8,128)(2,1)}), bf16[1024,2048]{1,0:T(8,128)(2,1)}) %all-gather.21.cloned.1.call-update) | async-done | bytes 4194320 | tf_op jit(solution)/shard_map/all_gather | solution.py:84
  260.3 8.7 multiply_convert_fusion.1
  269.0 45.8 %all-gather.23.cloned.1.call-done = bf16[2048,1024]{1,0:T(8,128)(2,1)} async-done(((bf16[2048,256]{1,0:T(8,128)(2,1)}), bf16[2048,1024]{1,0:T(8,128)(2,1)}) %all-gather.23.cloned.1.call-update) | async-done | bytes 4194320 | tf_op jit(solution)/shard_map/all_gather | solution.py:85
  322.8 16.9 %all-reduce.10.cloned.1.call-done = f32[256,1024]{1,0:T(8,128)} async-done(((f32[256,1024]{1,0:T(8,128)}), f32[256,1024]{1,0:T(8,128)}) %all-reduce.10.cloned.1.call-update) | async-done | bytes 1048592 | tf_op jit(solution)/shard_map/psum | solution.py:49
  350.2 20.9 %all-reduce.12.cloned.1.call-done = f32[256,1024]{1,0:T(8,128)} async-done(((f32[256,1024]{1,0:T(8,128)}), f32[256,1024]{1,0:T(8,128)}) %all-reduce.12.cloned.1.call-update) | async-done | bytes 1048592 | tf_op jit(solution)/shard_map/psum | solution.py:49
  376.0 35.6 %while.29 = (s32[]{:T(128)}, bf16[4,256,128]{1,2,0:T(8,128)(2,1)}, bf16[4,1024,128]{1,2,0:T(8,128)(2,1)}, bf16[4,1024,128]{1,2,0:T(8,128)(2,1)}, s32[4]{0:T(128)...) while((s32[]{:T(128)}, bf16[4,256,128]{1,2,0:T(8,128)(2,1)}, ...), condition=%wide.region_17.18_spmd.clone, body=%wide.region_15.17_spmd.clone.sunk | while | flops 339739136 | bytes 20001008 | solution.py:165
  415.7 21.7 %reduce-scatter.13.cloned.1.call-done = bf16[256,512]{0,1:T(8,128)(2,1)} async-done(((bf16[1024,512]{0,1:T(8,128)(2,1)}), bf16[256,512]{0,1:T(8,128)(2,1)}) %reduce-scatter.13.cloned.1.call-update) | async-done | bytes 262160 | tf_op jit(solution)/shard_map/reduce_scatter | solution.py:169
  439.8 25.7 %reduce-scatter.15.cloned.1.call-done = bf16[256,512]{0,1:T(8,128)(2,1)} async-done(((bf16[1024,512]{0,1:T(8,128)(2,1)}), bf16[256,512]{0,1:T(8,128)(2,1)}) %reduce-scatter.15.cloned.1.call-update) | async-done | bytes 262160 | tf_op jit(solution)/shard_map/reduce_scatter | solution.py:175
  487.0 9.9 %reduce-scatter.19.cloned.1.call-done = bf16[256,512]{0,1:T(8,128)(2,1)} async-done(((bf16[1024,512]{0,1:T(8,128)(2,1)}), bf16[256,512]{0,1:T(8,128)(2,1)}) %reduce-scatter.19.cloned.1.call-update) | async-done | bytes 262160 | tf_op jit(solution)/shard_map/reduce_scatter | solution.py:220
  496.9 30.5 %reduce-scatter.25.cloned.1.call-done = bf16[512,256]{1,0:T(8,128)(2,1)} async-done(((bf16[512,1024]{1,0:T(8,128)(2,1)}), bf16[512,256]{1,0:T(8,128)(2,1)}) %reduce-scatter.25.cloned.1.call-update) | async-done | bytes 262160 | tf_op jit(solution)/shard_map/reduce_scatter | solution.py:229
  527.4 31.3 %reduce-scatter.21.cloned.1.call-done = bf16[256,512]{0,1:T(8,128)(2,1)} async-done(((bf16[1024,512]{0,1:T(8,128)(2,1)}), bf16[256,512]{0,1:T(8,128)(2,1)}) %reduce-scatter.21.cloned.1.call-update) | async-done | bytes 262160 | tf_op jit(solution)/shard_map/reduce_scatter | solution.py:223
  558.8 30.5 %reduce-scatter.23.cloned.1.call-done = bf16[256,512]{0,1:T(8,128)(2,1)} async-done(((bf16[1024,512]{0,1:T(8,128)(2,1)}), bf16[256,512]{0,1:T(8,128)(2,1)}) %reduce-scatter.23.cloned.1.call-update) | async-done | bytes 262160 | tf_op jit(solution)/shard_map/reduce_scatter | solution.py:226
  589.3 55.8 %reduce-scatter.27.cloned.1.call-done = bf16[256,2048]{1,0:T(8,128)(2,1)} async-done(((bf16[1024,2048]{1,0:T(8,128)(2,1)}), bf16[256,2048]{1,0:T(8,128)(2,1)}) %reduce-scatter.27.cloned.1.call-update) | async-done | bytes 1048592 | tf_op jit(solution)/shard_map/reduce_scatter | solution.py:232
  645.1 55.6 %reduce-scatter.29.cloned.1.call-done = bf16[2048,256]{1,0:T(8,128)(2,1)} async-done(((bf16[2048,1024]{1,0:T(8,128)(2,1)}), bf16[2048,256]{1,0:T(8,128)(2,1)}) %reduce-scatter.29.cloned.1.call-update) | async-done | bytes 1048592 | tf_op jit(solution)/shard_map/reduce_scatter | solution.py:235
  709.9 17.6 %reduce-scatter.31.cloned.1.call-done = bf16[128,8]{1,0:T(8,128)(2,1)} async-done(((bf16[512,8]{1,0:T(8,128)(2,1)}), bf16[128,8]{1,0:T(8,128)(2,1)}) %reduce-scatter.31.cloned.1.call-update) | async-done | bytes 2064
  741.4 122.5 %all-reduce.14.cloned.1.call-done = (bf16[256,512]{0,1:T(8,128)(2,1)}, bf16[256,512]{0,1:T(8,128)(2,1)}, bf16[256,512]{0,1:T(8,128)(2,1)}, bf16[512,256]{1,0:T(8...) async-done(((bf16[256,512]{0,1:T(8,128)(2,1)}, bf16[256,512]{0,1:T(8,128)(2,1)}, bf16[256,512]{0,1:T(8,128)(2,1)}, bf16[512,256]{1,0:T(8,128)(2,1)}, ...) | async-done | bytes 3145744 | tf_op jit(solution)/shard_map/psum | solution.py:246
  (279 shorter events, 151.3 us)
Async XLA Ops:
  7.2 30.5 %all-gather.9.cloned.1.call-start = ((), (), s32[]{:S(2)}) async-start(), calls=%async_computation.10 | async-start | bytes 1310720 | tf_op jit(solution)/shard_map/all_gather | solution.py:82
  7.9 58.3 %all-gather.15.cloned.1.call-start = ((), (), s32[]{:S(2)}) async-start(), calls=%async_computation.13 | async-start | bytes 1310720 | tf_op jit(solution)/shard_map/all_gather | solution.py:81
  8.7 86.0 %all-gather.13.cloned.1.call-start = ((), (), s32[]{:S(2)}) async-start(), calls=%async_computation.12 | async-start | bytes 1310720 | tf_op jit(solution)/shard_map/all_gather | solution.py:80
  9.4 115.0 %all-gather.11.cloned.1.call-start = ((), (), s32[]{:S(2)}) async-start(), calls=%async_computation.11 | async-start | bytes 1310720 | tf_op jit(solution)/shard_map/all_gather | solution.py:99
  40.1 113.8 %all-gather.17.cloned.1.call-start = ((), (), s32[]{:S(2)}) async-start(), calls=%async_computation.14 | async-start | bytes 1310720 | tf_op jit(solution)/shard_map/all_gather | solution.py:98
  68.6 113.2 %all-gather.19.cloned.1.call-start = ((), (), s32[]{:S(2)}) async-start(), calls=%async_computation.15 | async-start | bytes 1310720 | tf_op jit(solution)/shard_map/all_gather | solution.py:83
  69.1 135.9 %all-reduce.8.cloned.1.call-start = ((), (), s32[]{:S(2)}) async-start(), calls=%async_computation.16 | async-start | bytes 2097152 | tf_op jit(solution)/shard_map/psum | solution.py:49
  184.5 75.8 %all-gather.21.cloned.1.call-start = ((), (), s32[]{:S(2)}) async-start(), calls=%async_computation.17 | async-start | bytes 5242880 | tf_op jit(solution)/shard_map/all_gather | solution.py:84
  185.3 129.6 %all-gather.23.cloned.1.call-start = ((), (), s32[]{:S(2)}) async-start(), calls=%async_computation.18 | async-start | bytes 5242880 | tf_op jit(solution)/shard_map/all_gather | solution.py:85
  186.0 153.7 %all-reduce.10.cloned.1.call-start = ((), (), s32[]{:S(2)}) async-start(), calls=%async_computation.19 | async-start | bytes 2097152 | tf_op jit(solution)/shard_map/psum | solution.py:49
  319.3 51.8 %all-reduce.12.cloned.1.call-start = ((), (), s32[]{:S(2)}) async-start(), calls=%async_computation.20 | async-start | bytes 2097152 | tf_op jit(solution)/shard_map/psum | solution.py:49
  350.1 87.2 %reduce-scatter.13.cloned.1.call-start = ((), (), s32[]{:S(2)}) async-start(), calls=%async_computation.21 | async-start | bytes 1310720 | tf_op jit(solution)/shard_map/reduce_scatter | solution.py:169
  411.6 53.9 %reduce-scatter.15.cloned.1.call-start = ((), (), s32[]{:S(2)}) async-start(), calls=%async_computation.22 | async-start | bytes 1310720 | tf_op jit(solution)/shard_map/reduce_scatter | solution.py:175
  412.4 84.5 %reduce-scatter.19.cloned.1.call-start = ((), (), s32[]{:S(2)}) async-start(), calls=%async_computation.24 | async-start | bytes 1310720 | tf_op jit(solution)/shard_map/reduce_scatter | solution.py:220
  414.2 113.3 %reduce-scatter.25.cloned.1.call-start = ((), (), s32[]{:S(2)}) async-start(), calls=%async_computation.27 | async-start | bytes 1310720 | tf_op jit(solution)/shard_map/reduce_scatter | solution.py:229
  415.7 143.1 %reduce-scatter.21.cloned.1.call-start = ((), (), s32[]{:S(2)}) async-start(), calls=%async_computation.25 | async-start | bytes 1310720 | tf_op jit(solution)/shard_map/reduce_scatter | solution.py:223
  439.8 149.5 %reduce-scatter.23.cloned.1.call-start = ((), (), s32[]{:S(2)}) async-start(), calls=%async_computation.26 | async-start | bytes 1310720 | tf_op jit(solution)/shard_map/reduce_scatter | solution.py:226
  467.9 177.2 %reduce-scatter.27.cloned.1.call-start = ((), (), s32[]{:S(2)}) async-start(), calls=%async_computation.28 | async-start | bytes 5242880 | tf_op jit(solution)/shard_map/reduce_scatter | solution.py:232
  472.6 228.2 %reduce-scatter.29.cloned.1.call-start = ((), (), s32[]{:S(2)}) async-start(), calls=%async_computation.29 | async-start | bytes 5242880 | tf_op jit(solution)/shard_map/reduce_scatter | solution.py:235
  478.3 249.2 %reduce-scatter.31.cloned.1.call-start = ((), (), s32[]{:S(2)}) async-start(), calls=%async_computation.30 | async-start | bytes 163840
  482.6 256.9 %reduce-scatter.17.cloned.1.call-start = ((), (), s32[]{:S(2)}) async-start(), calls=%async_computation.23 | async-start | bytes 786432 | tf_op jit(solution)/shard_map/reduce_scatter | solution.py:193
  486.9 214.0 %copy-start.22 = (u32[32]{0:T(128)S(1)}, u32[32]{0:T(128)}, u32[]{:S(2)}) copy-start(u32[32]{0:T(128)} %constant.147) | copy-start | bytes 388
  486.9 222.2 %copy-start.5 = (f32[256,1024]{1,0:T(8,128)S(1)}, f32[256,1024]{1,0:T(8,128)}, u32[]{:S(2)}) copy-start(f32[256,1024]{1,0:T(8,128)} %copy-done.4) | copy-start | bytes 3145732
  487.0 376.9 %all-reduce.14.cloned.1.call-start = ((), (), s32[]{:S(2)}) async-start(), calls=%async_computation.31 | async-start | bytes 6291456 | tf_op jit(solution)/shard_map/psum | solution.py:246
  (23 other events, 172.0 us)
Sparse Core Ops, SparseCore 0:
  9.9 27.7 all-gather.8
  39.5 26.6 all-gather.14
  68.0 26.6 all-gather.12
  96.7 27.6 all-gather.10
  126.4 27.4 all-gather.16
  155.5 26.2 all-gather.18
  184.7 20.3 all-reduce.7
  207.1 53.1 all-gather.20
  262.2 52.5 all-gather.22
  319.4 20.3 all-reduce.9
  350.3 20.7 all-reduce.11
  411.8 25.5 reduce-scatter.12
  439.7 25.7 reduce-scatter.14
  468.5 28.3 reduce-scatter.18
  499.7 27.7 reduce-scatter.24
  531.0 27.7 reduce-scatter.20
  561.5 27.7 reduce-scatter.22
  592.4 52.6 reduce-scatter.26
  648.1 52.6 reduce-scatter.28
  704.1 23.3 reduce-scatter.30
  730.3 9.1 reduce-scatter.16
  742.6 121.2 all-reduce.13
where the time goes:
time: 886 us; the launch traced here: 880 us
  waiting for transfers between devices  707 us (80%)
  matrix products  65.4 us (7%)
  local copies, waits for them, and re-layouts  40.8 us (5%)
  other arithmetic  23.2 us (3%)
  blocking collectives  21.5 us (2%)
  between operations  16.1 us (2%)
    psum x1, waiting for transfers between devices, per_device(): lax.psum(summed[0].astype(jnp.bfloat16), 'ctx').astype(jnp.float32)  122 us
    reduce_scatter x1, waiting for transfers between devices, per_device(): lax.psum_scatter(grad_parts[4].astype(jnp.bfloat16), 'fsdp', scatter_dime...  55.8 us
    reduce_scatter x1, waiting for transfers between devices, per_device(): lax.psum_scatter(grad_parts[5].astype(jnp.bfloat16), 'fsdp', scatter_dime...  55.6 us
    psum x3, waiting for transfers between devices, tensor_total(): return lax.psum(partial_rows, 'tp')  54.5 us
    all_gather x1, waiting for transfers between devices, per_device(): lax.all_gather(w_in, 'fsdp', axis=0, tiled=True)  53.5 us
    all_gather x1, waiting for transfers between devices, per_device(): lax.all_gather(w_down, 'fsdp', axis=1, tiled=True)  45.8 us
    reduce_scatter x1, waiting for transfers between devices, per_device(): lax.psum_scatter(grad_parts[1].astype(jnp.bfloat16), 'fsdp', scatter_dime...  31.3 us
    reduce_scatter x1, waiting for transfers between devices, per_device(): lax.psum_scatter(grad_parts[3].astype(jnp.bfloat16), 'fsdp', scatter_dime...  30.5 us
  transfers between devices with their start and end apart: 22, of which 22 were waited for; matrix products, arithmetic and copies ran while one was open for 7% of the time, Pallas kernels for 0%

commit v1 on v0

v1 whole, which is shorter than its diff:
```python
import functools

import jax
import jax.numpy as jnp
from jax import lax
from jax.experimental import pallas as pl
from jax.experimental.pallas import tpu as pltpu
from jax.sharding import PartitionSpec as P

HEAD = 64
MESH = pl.DeviceIdType.MESH

norm_eps = 1e-06
masked_score = -1e30


def matmul_plain(left_side, right_side):
    return jnp.dot(left_side, right_side, preferred_element_type=jnp.float32)


def matmul_left_t(left_side, right_side):
    return lax.dot_general(
        left_side, right_side, (((0,), (0,)), ((), ())), preferred_element_type=jnp.float32
    )


def matmul_right_t(left_side, right_side):
    return lax.dot_general(
        left_side, right_side, (((1,), (1,)), ((), ())), preferred_element_type=jnp.float32
    )


def norm_forward(values_in, gain_row, shift_row):
    center = values_in - jnp.mean(values_in, axis=-1, keepdims=True)
    spread = jnp.mean(center * center, axis=-1, keepdims=True)
    inv_dev = lax.rsqrt(spread + norm_eps)
    normed = center * inv_dev
    return (normed * gain_row + shift_row, normed, inv_dev)


def norm_backward(grad_out, gain_row, normed, inv_dev):
    grad_normed = grad_out * gain_row
    mean_plain = jnp.mean(grad_normed, axis=-1, keepdims=True)
    mean_normed = jnp.mean(grad_normed * normed, axis=-1, keepdims=True)
    return inv_dev * (grad_normed - mean_plain - normed * mean_normed)


def gelu_exact(values_in):
    return jax.nn.gelu(values_in, approximate=False)


def own_columns(matrix, tp_rank, half_width):
    return lax.dynamic_slice_in_dim(matrix, tp_rank * half_width, half_width, matrix.ndim - 1)


def greet(axis_peers):
    barrier = pltpu.get_barrier_semaphore()
    for peer in axis_peers:
        pl.semaphore_signal(barrier, inc=1, device_id=peer, device_id_type=MESH)
    pl.semaphore_wait(barrier, len(axis_peers))


def remote(src, dst, send_sem, recv_sem, peer):
    return pltpu.make_async_remote_copy(
        src_ref=src,
        dst_ref=dst,
        send_sem=send_sem,
        recv_sem=recv_sem,
        device_id=peer,
        device_id_type=MESH,
    )


def gather_kernel(n, x_ref, out_ref, send_sem, recv_sem, pair_send, pair_recv, own_sem):
    c_rank = lax.axis_index("ctx")
    t_rank = lax.axis_index("tp")
    rows, half = x_ref.shape
    sibling = {"tp": 1 - t_rank}

    def place(c_index, t_index):
        return out_ref.at[
            pl.ds(pl.multiple_of(c_index * rows, rows), rows),
            pl.ds(pl.multiple_of(t_index * half, half), half),
        ]

    greet([{"ctx": lax.rem(c_rank + k, n)} for k in range(1, n)] + [sibling])
    own = place(c_rank, t_rank)
    sends = [
        remote(x_ref, own, send_sem.at[k], recv_sem.at[k], {"ctx": lax.rem(c_rank + k, n)})
        for k in range(1, n)
    ]
    for send in sends:
        send.start()
    pair = [remote(x_ref, own, pair_send.at[0], pair_recv.at[0], sibling)]
    pair[0].start()
    keep = pltpu.make_async_copy(x_ref, own, own_sem)
    keep.start()
    for k in range(1, n):
        spot = place(lax.rem(c_rank + n - k, n), t_rank)
        remote(x_ref, spot, send_sem.at[k], recv_sem.at[k], sibling).wait_recv()
        relay = remote(spot, spot, pair_send.at[k], pair_recv.at[k], sibling)
        relay.start()
        pair.append(relay)
    keep.wait()
    for send in sends:
        send.wait_send()
    for k in range(n):
        pair[k].wait_send()
        spot = place(lax.rem(c_rank + n - k, n), 1 - t_rank)
        remote(x_ref, spot, pair_send.at[k], pair_recv.at[k], sibling).wait_recv()


def gather_rows(own_half, n):
    rows, half = own_half.shape
    return pl.pallas_call(
        functools.partial(gather_kernel, n),
        out_shape=jax.ShapeDtypeStruct((n * rows, 2 * half), own_half.dtype),
        in_specs=[pl.BlockSpec(memory_space=pl.ANY)],
        out_specs=pl.BlockSpec(memory_space=pl.ANY),
        scratch_shapes=[
            pltpu.SemaphoreType.DMA((n,)),
            pltpu.SemaphoreType.DMA((n,)),
            pltpu.SemaphoreType.DMA((n,)),
            pltpu.SemaphoreType.DMA((n,)),
            pltpu.SemaphoreType.DMA,
        ],
        compiler_params=pltpu.CompilerParams(collective_id=0, has_side_effects=True),
        name="gather_rows",
    )(own_half)


def scatter_kernel(
    n,
    share,
    a_ref,
    b_ref,
    out_ref,
    mine,
    give,
    take,
    z_give,
    z_take,
    give_sem,
    take_sem,
    z_give_sem,
    z_take_sem,
    out_sems,
):
    c_rank = lax.axis_index("ctx")
    t_rank = lax.axis_index("tp")
    rows, half = mine.shape[1], mine.shape[2]
    sibling = {"tp": 1 - t_rank}
    greet([{"ctx": lax.rem(c_rank + k, n)} for k in range(1, n)] + [sibling])
    order = list(range(1, n)) + [0]

    def column_part(block, t_index):
        weight = b_ref[pl.ds(pl.multiple_of(t_index * half, half), half), :]
        return matmul_right_t(block, weight)

    pair = {}
    for k in order:
        target = lax.rem(c_rank + k, n)
        block = a_ref[pl.ds(pl.multiple_of(target * rows, rows), rows), :]
        give[k] = column_part(block, 1 - t_rank).astype(give.dtype)
        pair[k] = remote(give.at[k], take.at[k], give_sem.at[k], take_sem.at[k], sibling)
        pair[k].start()
        mine[k] = column_part(block, t_rank)
    sends = {}
    for k in order:
        pair[k].wait_recv()
        if k > 0:
            z_give[k] = (mine[k] + take[k].astype(jnp.float32)).astype(z_give.dtype)
            sends[k] = remote(
                z_give.at[k],
                z_take.at[k],
                z_give_sem.at[k],
                z_take_sem.at[k],
                {"ctx": lax.rem(c_rank + k, n)},
            )
            sends[k].start()
    total = mine[0] + take[0].astype(jnp.float32)
    for k in range(1, n):
        sends[k].wait_recv()
        total = total + z_take[k].astype(jnp.float32)
    if share:
        out_ref[t_rank] = total
        last = remote(
            out_ref.at[t_rank], out_ref.at[t_rank], out_sems.at[0], out_sems.at[1], sibling
        )
        last.start()
        last.wait_send()
        remote(
            out_ref.at[t_rank], out_ref.at[1 - t_rank], out_sems.at[0], out_sems.at[1], sibling
        ).wait_recv()
    else:
        out_ref[0] = total
    for k in order:
        pair[k].wait_send()
    for k in range(1, n):
        sends[k].wait_send()


def scatter_rows(left, right, n, share, kernel_id):
    rows, half = left.shape[0] // n, right.shape[0] // 2
    parts = 2 if share else 1
    blocks = (n, rows, half)
    sem = pltpu.SemaphoreType.DMA((n,))
    return pl.pallas_call(
        functools.partial(scatter_kernel, n, share),
        out_shape=jax.ShapeDtypeStruct((parts, rows, half), jnp.float32),
        in_specs=[pl.BlockSpec(memory_space=pltpu.VMEM)] * 2,
        out_specs=pl.BlockSpec(memory_space=pltpu.VMEM),
        scratch_shapes=[
            pltpu.VMEM(blocks, jnp.float32),
            pltpu.VMEM(blocks, jnp.bfloat16),
            pltpu.VMEM(blocks, jnp.bfloat16),
            pltpu.VMEM(blocks, jnp.bfloat16),
            pltpu.VMEM(blocks, jnp.bfloat16),
            sem,
            sem,
            sem,
            sem,
            pltpu.SemaphoreType.DMA((2,)),
        ],
        compiler_params=pltpu.CompilerParams(
            collective_id=kernel_id, has_side_effects=True, vmem_limit_bytes=40 * 2**20
        ),
        name="scatter_rows",
    )(left, right)


def whole_rows(parts):
    return jnp.concatenate([parts[0], parts[1]], axis=1)


def per_device(
    tokens, w_query, w_key, w_value, w_attn_out, w_in, w_down, vectors, bias_in, lengths, cotangent
):
    row_count, half_width = tokens.shape
    tp_rank = lax.axis_index("tp")
    ctx_rank = lax.axis_index("ctx")
    ctx_size = lax.axis_size("ctx")
    seq_slots = row_count * ctx_size
    head_width = half_width // ctx_size
    heads = head_width // HEAD
    unit_count = w_in.shape[1] // ctx_size

    def own_share(matrix, width, axis):
        return lax.dynamic_slice_in_dim(matrix, ctx_rank * width, width, axis)

    attn_pack = jnp.concatenate(
        [own_share(matrix, head_width, 1) for matrix in (w_query, w_key, w_value)]
        + [own_share(w_attn_out, head_width, 0).T],
        axis=1,
    )
    ffn_pack = jnp.concatenate(
        [own_share(w_in, unit_count, 1), own_share(w_down, unit_count, 0).T], axis=1
    )
    w_attn = lax.all_gather(attn_pack, "fsdp", axis=0, tiled=True)
    w_ffn = lax.all_gather(ffn_pack, "fsdp", axis=0, tiled=True)
    w_qkv, w_o = w_attn[:, : 3 * head_width], w_attn[:, 3 * head_width :]
    w_i, w_d = w_ffn[:, :unit_count], w_ffn[:, unit_count:]

    tok_seq = gather_rows(tokens, ctx_size)
    vec_rows = lax.all_gather(vectors, "tp", axis=1, tiled=True).astype(jnp.float32)
    cot_full = lax.all_gather(cotangent, "tp", axis=1, tiled=True)
    tok_float = lax.dynamic_slice_in_dim(tok_seq, ctx_rank * row_count, row_count, 0).astype(
        jnp.float32
    )
    head_vec = own_share(vectors, head_width, 1).astype(jnp.float32)
    unit_bias = own_share(bias_in, unit_count, 0).astype(jnp.float32)
    seq_length = lengths[0]
    key_valid = jnp.arange(seq_slots) < seq_length
    row_valid = ctx_rank * row_count + jnp.arange(row_count) < seq_length
    seed_grad = cot_full.astype(jnp.float32) * row_valid[:, None].astype(jnp.float32)

    def split_heads(matrix):
        return matrix.reshape(seq_slots, heads, HEAD)

    projected = matmul_plain(tok_seq, w_qkv)
    queries = ((projected[:, :head_width] + head_vec[0]) * 0.125).astype(jnp.bfloat16)
    keys = projected[:, head_width : 2 * head_width].astype(jnp.bfloat16)
    values = (projected[:, 2 * head_width :] + head_vec[1]).astype(jnp.bfloat16)
    head_q, head_k, head_v = split_heads(queries), split_heads(keys), split_heads(values)
    scores = jnp.einsum("qhd,khd->hqk", head_q, head_k, preferred_element_type=jnp.float32)
    scores = jnp.where(key_valid[None, None, :], scores, masked_score)
    top_score = jnp.max(scores, axis=-1, keepdims=True)
    weights_exp = jnp.exp(scores - top_score)
    probs = weights_exp / jnp.sum(weights_exp, axis=-1, keepdims=True)
    probs_low = probs.astype(jnp.bfloat16)
    mixed = jnp.einsum("hqk,khd->qhd", probs_low, head_v, preferred_element_type=jnp.float32)
    context = mixed.reshape(seq_slots, head_width).astype(jnp.bfloat16)

    attended = whole_rows(scatter_rows(context, w_o, ctx_size, True, 1))
    hidden_one, normed_one, inv_one = norm_forward(
        tok_float + attended + vec_rows[2], vec_rows[4], vec_rows[5]
    )
    hidden_seq = gather_rows(
        own_columns(hidden_one, tp_rank, half_width).astype(jnp.bfloat16), ctx_size
    )
    pre_act = matmul_plain(hidden_seq, w_i) + unit_bias
    activated, gelu_pull = jax.vjp(gelu_exact, pre_act)
    act_low = activated.astype(jnp.bfloat16)
    branch = whole_rows(scatter_rows(act_low, w_d, ctx_size, True, 2))
    layer_out, normed_two, inv_two = norm_forward(
        hidden_one + branch + vec_rows[3], vec_rows[6], vec_rows[7]
    )
    output_rows = own_columns(layer_out, tp_rank, half_width).astype(jnp.bfloat16)
    grad_two = norm_backward(seed_grad, vec_rows[6], normed_two, inv_two)
    branch_seq = gather_rows(
        own_columns(grad_two, tp_rank, half_width).astype(jnp.bfloat16), ctx_size
    )
    pre_low = gelu_pull(matmul_plain(branch_seq, w_d))[0].astype(jnp.bfloat16)
    grad_hidden = grad_two + whole_rows(scatter_rows(pre_low, w_i, ctx_size, True, 3))
    grad_one = norm_backward(grad_hidden, vec_rows[4], normed_one, inv_one)
    attn_seq = gather_rows(
        own_columns(grad_one, tp_rank, half_width).astype(jnp.bfloat16), ctx_size
    )

    def share_gradient(pack):
        own_rows = lax.psum_scatter(
            pack.astype(jnp.bfloat16), "fsdp", scatter_dimension=0, tiled=True
        )
        return lax.all_gather(own_rows, "ctx", axis=0).astype(jnp.float32)

    ffn_grads = share_gradient(
        jnp.concatenate(
            [matmul_left_t(hidden_seq, pre_low), matmul_left_t(branch_seq, act_low)], axis=1
        )
    )

    grad_context = matmul_plain(attn_seq, w_o).astype(jnp.bfloat16)
    head_g = split_heads(grad_context)
    grad_probs = jnp.einsum("qhd,khd->hqk", head_g, head_v, preferred_element_type=jnp.float32)
    inner = jnp.sum(probs * grad_probs, axis=-1, keepdims=True)
    grad_scores = (probs * (grad_probs - inner)).astype(jnp.bfloat16)
    grad_q = jnp.einsum("hqk,khd->qhd", grad_scores, head_k, preferred_element_type=jnp.float32)
    grad_k = jnp.einsum("hqk,qhd->khd", grad_scores, head_q, preferred_element_type=jnp.float32)
    grad_v = jnp.einsum("hqk,qhd->khd", probs_low, head_g, preferred_element_type=jnp.float32)
    qkv_low = jnp.concatenate(
        [
            grad_q.reshape(seq_slots, head_width).astype(jnp.bfloat16) * 0.125,
            grad_k.reshape(seq_slots, head_width).astype(jnp.bfloat16),
            grad_v.reshape(seq_slots, head_width).astype(jnp.bfloat16),
        ],
        axis=1,
    )
    attn_grads = share_gradient(
        jnp.concatenate(
            [matmul_left_t(tok_seq, qkv_low), matmul_left_t(attn_seq, context)], axis=1
        )
    )
    grad_tokens = scatter_rows(qkv_low, w_qkv, ctx_size, False, 4)[0] + own_columns(
        grad_one, tp_rank, half_width
    )

    def spread(row, width):
        return lax.dynamic_update_slice_in_dim(
            jnp.zeros((width,), jnp.float32), row, ctx_rank * row.shape[0], 0
        )

    column_sums = jnp.sum(qkv_low.astype(jnp.float32), axis=0)
    small_grads = jnp.concatenate(
        [
            spread(column_sums[:head_width], half_width),
            spread(column_sums[2 * head_width :], half_width),
            own_columns(jnp.sum(grad_one, axis=0), tp_rank, half_width),
            own_columns(jnp.sum(grad_two, axis=0), tp_rank, half_width),
            own_columns(jnp.sum(grad_hidden * normed_one, axis=0), tp_rank, half_width),
            own_columns(jnp.sum(grad_hidden, axis=0), tp_rank, half_width),
            own_columns(jnp.sum(seed_grad * normed_two, axis=0), tp_rank, half_width),
            own_columns(jnp.sum(seed_grad, axis=0), tp_rank, half_width),
            spread(jnp.sum(pre_low.astype(jnp.float32), axis=0), unit_count * ctx_size),
        ]
    )
    small_total = lax.psum(small_grads, ("fsdp", "ctx"))
    fsdp_rank = lax.axis_index("fsdp")
    fsdp_size = lax.axis_size("fsdp")
    vector_grads = own_columns(
        small_total[: 8 * half_width].reshape(8, half_width), fsdp_rank, half_width // fsdp_size
    )
    bias_width = unit_count * ctx_size // fsdp_size
    bias_grad = own_columns(small_total[8 * half_width :], fsdp_rank, bias_width)

    def side_by_side(blocks):
        return blocks.transpose(1, 0, 2).reshape(blocks.shape[1], -1)

    def stacked(blocks):
        return blocks.transpose(0, 2, 1).reshape(-1, blocks.shape[1])

    return (
        output_rows,
        grad_tokens,
        side_by_side(attn_grads[:, :, :head_width]),
        side_by_side(attn_grads[:, :, head_width : 2 * head_width]),
        side_by_side(attn_grads[:, :, 2 * head_width : 3 * head_width]),
        stacked(attn_grads[:, :, 3 * head_width :]),
        side_by_side(ffn_grads[:, :, :unit_count]),
        stacked(ffn_grads[:, :, unit_count:]),
        vector_grads,
        bias_grad,
    )


def solution(mesh):
    placed = (
        P(("fsdp", "ctx"), "tp"),
        P("fsdp", "tp"),
        P("fsdp", "tp"),
        P("fsdp", "tp"),
        P("tp", "fsdp"),
        P("fsdp", "tp"),
        P("tp", "fsdp"),
        P(None, "tp"),
        P("tp"),
        P("fsdp"),
        P(("fsdp", "ctx"), "tp"),
    )
    return jax.shard_map(
        per_device,
        mesh=mesh,
        in_specs=placed,
        out_specs=(
            P(("fsdp", "ctx"), "tp"),
            P(("fsdp", "ctx"), "tp"),
            P("fsdp", "tp"),
            P("fsdp", "tp"),
            P("fsdp", "tp"),
            P("tp", "fsdp"),
            P("fsdp", "tp"),
            P("tp", "fsdp"),
            P(None, ("tp", "fsdp")),
            P(("tp", "fsdp")),
        ),
        check_vma=False,
    )
```

time: 886 us -> 508 us (0.57)
  waiting for transfers between devices: 707 us -> 61.7 us
  Pallas kernels: 0 us -> 250 us
  blocking collectives: 21.5 us -> 65.4 us
  matrix products: 65.4 us -> 45.8 us
    pallas_call x0 -> x8, Pallas kernels: none -> 250 us  [the longest x4 137 us: scatter_rows(): pl.pallas_call(functools.partial(scatter_kernel, n, share), out_shape=jax...]
    all_gather x8 -> x4, waiting for transfers between devices: 243 us -> 0.05 us  [the longest x1 0.02 us: per_device(): w_attn = lax.all_gather(attn_pack, 'fsdp', axis=0, tiled=True)]
    reduce_scatter x9 -> x2, waiting for transfers between devices: 264 us -> 61.6 us  [share_gradient(): lax.psum_scatter(pack.astype(jnp.bfloat16), 'fsdp', scatter_dimension=0,...]
    psum x4 -> x0, waiting for transfers between devices: 177 us -> none  [the longest x1 122 us: per_device(): lax.psum(summed[0].astype(jnp.bfloat16), 'ctx').astype(jnp.float32)]
    psum x1, blocking collectives: 6.88 us -> 60.9 us  [per_device(): small_total = lax.psum(small_grads, ('fsdp', 'ctx'))]
    unnamed x23 -> x6, waiting for transfers between devices: 22.5 us -> 0.1 us
    dot_general x34 -> x5, matrix products: 26.5 us -> 13 us  [the longest x1 4.91 us: per_device(): jnp.einsum('hqk,qhd->khd', probs_low, head_g, preferred_element_type=jnp....]
    dynamic_slice x36 -> x5, local copies, waits for them, and re-layouts: 16.6 us -> 3.66 us  [own_share(): return lax.dynamic_slice_in_dim(matrix, ctx_rank * width, width, axis)]
  transfers between devices with their start and end apart: 22 -> 6, of which waited for: 22 -> 2; matrix products, arithmetic and copies ran while one was open for 7% -> 8% of each run, Pallas kernels for 0% -> 26%
where the time goes in v1:
time: 508 us; the launch traced here: 499 us
  Pallas kernels  250 us (49%)
  blocking collectives  65.4 us (13%)
  waiting for transfers between devices  61.7 us (12%)
  matrix products  45.8 us (9%)
  local copies, waits for them, and re-layouts  43.8 us (9%)
  other arithmetic  16 us (3%)
  between operations  16 us (3%)
    pallas_call x4, Pallas kernels, scatter_rows(): pl.pallas_call(functools.partial(scatter_kernel, n, share), out_shape=jax...  137 us
    pallas_call x4, Pallas kernels, gather_rows(): pl.pallas_call(functools.partial(gather_kernel, n), out_shape=jax.ShapeDt...  114 us
    reduce_scatter x2, waiting for transfers between devices, share_gradient(): lax.psum_scatter(pack.astype(jnp.bfloat16), 'fsdp', scatter_dimension=0,...  61.6 us
    psum x1, blocking collectives, per_device(): small_total = lax.psum(small_grads, ('fsdp', 'ctx'))  60.9 us
    dot_general x4, matrix products, matmul_plain(): return jnp.dot(left_side, right_side, preferred_element_type=jnp.float32)  17 us
    unnamed x66, local copies, waits for them, and re-layouts  10.5 us
  transfers between devices with their start and end apart: 6, of which 2 were waited for; matrix products, arithmetic and copies ran while one was open for 8% of the time, Pallas kernels for 26%

profile of v1, /device:TPU:9, one launch (start us, length us, event | category | flops | bytes accessed | tf_op | source)
XLA Modules:
  0.0 499.2 jit_solution(17804060413537884846)
XLA Ops:
  19.0 28.6 %gather_rows.4 = bf16[1024,1024]{1,0:T(8,128)(2,1)} custom-call(bf16[256,512]{1,0:T(8,128)(2,1)} %x_ref.1), custom_call_target="tpu_custom_call" | custom-call | tf_op jit(solution)/shard_map/gather_rows/pallas_call | solution.py:115
  47.6 3.0 convolution_bitcast_fusion
  50.9 6.0 %fusion.55 = (f32[2,1024]{1,0:T(2,128)S(1)}, f32[2,1024,1024]{1,2,0:T(8,128)}) fusion(pred[1024]{0:T(1024)(128)(4,1)S(1)} %iota_compare_fusion, bf16[1024,2,64]{0,2,1:T(8,128)(2,1)S(1)} %bitcast.119, bf16[1024,2,64]{0,2,1:T(8,128)(2,1)S(1)} %bitcast.108), kind=kOutput, calls=%fused_computation.145 | convolution fusion | flops 274727936 | bytes 8922112 | tf_op jit(solution)/shard_map/sub | solution.py:288
  56.9 4.2 fusion.17
  62.9 30.0 %scatter_rows.4 = f32[2,256,512]{2,1,0:T(8,128)S(1)} custom-call(bf16[1024,128]{1,0:T(8,128)(2,1)S(1)} %copy.39.a_ref, bf16[1024,128]{1,0:T(8,128)(2,1)S(1)} %slice.142.b_ref), custom_call_target="tpu_custom_call" | custom-call | tf_op jit(solution)/shard_map/scatter_rows/pallas_call | solution.py:208
  95.6 28.4 %gather_rows.5 = bf16[1024,1024]{1,0:T(8,128)(2,1)} custom-call(bf16[256,512]{1,0:T(8,128)(2,1)} %dynamic-slice_convert_fusion.1.x_ref), custom_call_target="tpu_custom_call" | custom-call | tf_op jit(solution)/shard_map/gather_rows/pallas_call | solution.py:115
  126.9 6.9 %multiply_convert_fusion.1 = (bf16[1024,512]{1,0:T(8,128)(2,1)S(1)}, f32[1024,512]{1,0:T(8,128)}, f32[1024,512]{1,0:T(8,128)}) fusion(f32[512]{0:T(512)S(1)} %dynamic-slice_convert_fusion.3, bf16[1024,1024]{1,0:T(8,128)(2,1)S(1)} %copy-done.11, bf16[1024,1024]{1,0:T(8,128)(2,1)S(1)} %copy-done.13), kind=kOutput, calls=%fused_computation.16 | convolution fusion | flops 1108344832 | bytes 8390656 | tf_op jit(solution)/shard_map/dot_general | solution.py:18
  133.9 30.7 %scatter_rows.5 = f32[2,256,512]{2,1,0:T(8,128)S(1)} custom-call(bf16[1024,512]{1,0:T(8,128)(2,1)S(1)} %get-tuple-element.28.a_ref, bf16[1024,512]{1,0:T(8,128)(2,1)S(1)} %get-tuple-element.39.b_ref), custom_call_target="tpu_custom_call" | custom-call | tf_op jit(solution)/shard_map/scatter_rows/pallas_call | solution.py:208
  169.4 28.4 %gather_rows.6 = bf16[1024,1024]{1,0:T(8,128)(2,1)} custom-call(bf16[256,512]{1,0:T(8,128)(2,1)} %dynamic-slice_convert_fusion.x_ref), custom_call_target="tpu_custom_call" | custom-call | tf_op jit(solution)/shard_map/gather_rows/pallas_call | solution.py:115
  197.8 5.1 %convert_reduce_fusion = (f32[512]{0:T(512)S(1)}, bf16[1024,512]{1,0:T(8,128)(2,1)S(1)}) fusion(f32[1024,512]{1,0:T(8,128)} %get-tuple-element.29, bf16[1024,1024]{1,0:T(8,128)(2,1)} %gather_rows.6, bf16[1024,1024]{1,0:T(8,128)(2,1)} %all-gather.9.cloned.1.call-done, f32[1024,512]{1,0:T(8,128)} %get-tuple-element.58, f32[512]{0:T(512)S(1)} %dynamic-slice_convert_fusion.3), kind=kOutput, calls=%fused_computation.14 | convolution fusion | flops 1082654208 | bytes 8392704 | tf_op jit(solution)/shard_map/dot_general | solution.py:18
  202.9 30.6 %scatter_rows.6 = f32[2,256,512]{2,1,0:T(8,128)S(1)} custom-call(bf16[1024,512]{1,0:T(8,128)(2,1)S(1)} %get-tuple-element.62.a_ref, bf16[1024,512]{1,0:T(8,128)(2,1)S(1)} %get-tuple-element.38.b_ref), custom_call_target="tpu_custom_call" | custom-call | tf_op jit(solution)/shard_map/scatter_rows/pallas_call | solution.py:208
  236.3 28.4 %gather_rows.7 = bf16[1024,1024]{1,0:T(8,128)(2,1)} custom-call(bf16[256,512]{1,0:T(8,128)(2,1)} %dynamic-slice_convert_fusion.2.x_ref), custom_call_target="tpu_custom_call" | custom-call | tf_op jit(solution)/shard_map/gather_rows/pallas_call | solution.py:115
  264.7 2.9 convolution_convert_fusion.3
  269.5 4.9 fusion.20
  276.1 2.7 multiply_convert_fusion
  283.5 2.6 fusion.16
  287.3 3.0 convolution_convert_fusion
  293.2 22.8 %reduce-scatter.3.cloned.1.call-done = bf16[256,512]{0,1:T(8,128)(2,1)} async-done(((bf16[1024,512]{0,1:T(8,128)(2,1)}), bf16[256,512]{0,1:T(8,128)(2,1)}) %reduce-scatter.3.cloned.1.call-update) | async-done | bytes 262160 | tf_op jit(solution)/shard_map/reduce_scatter | solution.py:321
  316.1 38.8 %reduce-scatter.5.cloned.1.call-done = bf16[256,1024]{0,1:T(8,128)(2,1)} async-done(((bf16[1024,1024]{0,1:T(8,128)(2,1)}), bf16[256,1024]{0,1:T(8,128)(2,1)}) %reduce-scatter.5.cloned.1.call-update) | async-done | bytes 524304 | tf_op jit(solution)/shard_map/reduce_scatter | solution.py:321
  357.3 60.9 %psum.7 = f32[6144]{0:T(1024)S(1)} all-reduce(f32[6144]{0:T(1024)S(1)} %constant_dynamic-update-slice_fusion), channel_id=1, replica_groups=mesh['fsdp'=4,'ctx'=4,'tp'=2] {'fsdp','ctx'}, use_global_device_ids=true, to_apply=%region_21.22 | all-reduce | flops 6144 | bytes 49152 | tf_op jit(solution)/shard_map/psum | solution.py:376
  418.2 45.2 %scatter_rows.7 = f32[1,256,512]{2,1,0:T(8,128)S(1)} custom-call(bf16[1024,384]{1,0:T(8,128)(2,1)S(1)} %get-tuple-element.23.a_ref, bf16[1024,384]{1,0:T(8,128)(2,1)S(1)} %slice.138.b_ref), custom_call_target="tpu_custom_call" | custom-call | tf_op jit(solution)/shard_map/scatter_rows/pallas_call | solution.py:208
  475.9 5.0 %reshape.137 = f32[4,256,1024]{1,0,2:T(4,128)} reshape(bf16[1024,1024]{0,1:T(8,128)(2,1)} %all-gather.13.cloned.1.call-done) | data formatting | bytes 6291456 | tf_op jit(solution)/shard_map/convert_element_type | solution.py:324
  480.9 4.3 slice_bitcast_fusion
  486.8 2.9 copy.51
  (162 shorter events, 56.9 us)
Async XLA Ops:
  7.2 3.7 copy-start
  7.2 40.4 %all-gather.7.cloned.1.call-start = ((), (), s32[]{:S(2)}) async-start(), calls=%async_computation.2 | async-start | bytes 1310720 | tf_op jit(solution)/shard_map/all_gather | solution.py:259
  9.1 3.8 copy-start.23
  10.0 6.6 %copy-start.20 = (bf16[256,512]{1,0:T(8,128)(2,1)S(1)}, bf16[256,512]{1,0:T(8,128)(2,1)}, u32[]{:S(2)}) copy-start(bf16[256,512]{1,0:T(8,128)(2,1)} %param.21) | copy-start | bytes 786436
  10.8 113.2 %all-gather.9.cloned.1.call-start = ((), (), s32[]{:S(2)}) async-start(), calls=%async_computation.3 | async-start | bytes 2621440 | tf_op jit(solution)/shard_map/all_gather | solution.py:260
  12.9 303.1 %reduce-scatter.3.cloned.1.call-start = ((), (), s32[]{:S(2)}) async-start(), calls=%async_computation.4 | async-start | bytes 1310720 | tf_op jit(solution)/shard_map/reduce_scatter | solution.py:321
  50.8 6.0 %copy-start.17 = (bf16[1024,128]{0,1:T(8,128)(2,1)}, bf16[1024,128]{0,1:T(8,128)(2,1)S(1)}, u32[]{:S(2)}) copy-start(bf16[1024,128]{0,1:T(8,128)(2,1)S(1)} %get-tuple-element.40) | copy-start | bytes 786436
  50.8 6.0 %copy-start.21 = (bf16[1024,128]{0,1:T(8,128)(2,1)}, bf16[1024,128]{0,1:T(8,128)(2,1)S(1)}, u32[]{:S(2)}) copy-start(bf16[1024,128]{0,1:T(8,128)(2,1)S(1)} %get-tuple-element.41) | copy-start | bytes 786436
  94.3 70.3 %copy-start.2 = (f32[256,1024]{1,0:T(8,128)}, f32[256,1024]{1,0:T(8,128)S(1)}, u32[]{:S(2)}) copy-start(f32[256,1024]{1,0:T(8,128)S(1)} %get-tuple-element.31) | copy-start | bytes 3145732
  124.1 2.8 copy-start.13
  202.9 30.8 %copy-start.3 = (f32[256,1024]{1,0:T(8,128)S(1)}, f32[256,1024]{1,0:T(8,128)}, u32[]{:S(2)}) copy-start(f32[256,1024]{1,0:T(8,128)} %copy-done.2) | copy-start | bytes 3145732
  202.9 30.8 %copy-start.8 = (f32[256,1024]{1,0:T(8,128)S(1)}, f32[256,1024]{1,0:T(8,128)}, u32[]{:S(2)}) copy-start(f32[256,1024]{1,0:T(8,128)} %copy-done.7) | copy-start | bytes 3145732
  234.6 30.1 %copy-start.16 = (bf16[2,64,1024]{2,1,0:T(8,128)(2,1)S(1)}, bf16[2,64,1024]{2,1,0:T(8,128)(2,1)}, u32[]{:S(2)}) copy-start(bf16[2,64,1024]{2,1,0:T(8,128)(2,1)} %copy-done.15) | copy-start | bytes 786436
  264.7 2.9 copy-start.4
  267.6 6.9 %slice-start = ((s8[8388608]{0:T(1024)(128)(4,1)}), s8[4194304]{0:T(1024)(128)(4,1)S(1)}, s32[]{:S(2)}) async-start(s8[8388608]{0:T(1024)(128)(4,1)} %bitcast.105), calls=%async_computation.8 | async-start | bytes 8388608
  269.5 5.0 slice-start.1
  269.5 5.0 copy-start.22
  276.1 2.7 copy-start.18
  287.2 67.6 %reduce-scatter.5.cloned.1.call-start = ((), (), s32[]{:S(2)}) async-start(), calls=%async_computation.5 | async-start | bytes 2621440 | tf_op jit(solution)/shard_map/reduce_scatter | solution.py:321
  287.3 3.0 copy-start.12
  293.2 174.2 %all-gather.11.cloned.1.call-start = ((), (), s32[]{:S(2)}) async-start(), calls=%async_computation.6 | async-start | bytes 1310720 | tf_op jit(solution)/shard_map/all_gather | solution.py:324
  316.0 159.9 %all-gather.13.cloned.1.call-start = ((), (), s32[]{:S(2)}) async-start(), calls=%async_computation.7 | async-start | bytes 2621440 | tf_op jit(solution)/shard_map/all_gather | solution.py:324
  354.9 109.8 %copy-start.6 = (f32[256,1024]{1,0:T(8,128)S(1)}, f32[256,1024]{1,0:T(8,128)}, u32[]{:S(2)}) copy-start(f32[256,1024]{1,0:T(8,128)} %copy-done.5) | copy-start | bytes 3145732
  470.7 3.0 copy-start.14
  (8 other events, 11.8 us)
Sparse Core Ops, SparseCore 0:
  10.9 27.7 all-gather.6
  41.2 35.2 all-gather.8
  287.3 28.6 reduce-scatter.2
  319.7 35.1 reduce-scatter.4
  356.3 27.7 all-gather.10
  385.5 46.6 all-gather.12

commit v2 on v1

--- a/solution.py
+++ b/solution.py
@@ -53,11 +53,29 @@
     return lax.dynamic_slice_in_dim(matrix, tp_rank * half_width, half_width, matrix.ndim - 1)
 
 
-def greet(axis_peers):
+def greet(n, axes):
     barrier = pltpu.get_barrier_semaphore()
-    for peer in axis_peers:
+    c_rank = lax.axis_index("ctx")
+
+    def hail(peer):
         pl.semaphore_signal(barrier, inc=1, device_id=peer, device_id_type=MESH)
-    pl.semaphore_wait(barrier, len(axis_peers))
+
+    @pl.when(c_rank > 0)
+    def _():
+        hail({"ctx": c_rank - 1})
+
+    @pl.when(c_rank < n - 1)
+    def _():
+        hail({"ctx": c_rank + 1})
+
+    hail({"tp": 1 - lax.axis_index("tp")})
+    others = 1
+    for axis, size in axes:
+        for k in range(1, size):
+            hail({axis: lax.rem(lax.axis_index(axis) + k, size)})
+        others += size - 1
+    edge = jnp.where(c_rank > 0, 1, 0) + jnp.where(c_rank < n - 1, 1, 0)
+    pl.semaphore_wait(barrier, others + edge)
 
 
 def remote(src, dst, send_sem, recv_sem, peer):
@@ -71,7 +89,7 @@
     )
 
 
-def gather_kernel(n, x_ref, out_ref, send_sem, recv_sem, pair_send, pair_recv, own_sem):
+def gather_kernel(n, x_ref, out_ref, send_r, recv_r, send_l, recv_l, pair_send, pair_recv, own_sem):
     c_rank = lax.axis_index("ctx")
     t_rank = lax.axis_index("tp")
     rows, half = x_ref.shape
@@ -83,31 +101,69 @@
             pl.ds(pl.multiple_of(t_index * half, half), half),
         ]
 
-    greet([{"ctx": lax.rem(c_rank + k, n)} for k in range(1, n)] + [sibling])
+    def to_side(step, sign):
+        spot = place(c_rank - sign * step, t_rank)
+        send, recv = (send_r, recv_r) if sign > 0 else (send_l, recv_l)
+        source = x_ref if step == 0 else spot
+        return remote(source, spot, send.at[step], recv.at[step], {"ctx": c_rank + sign})
+
+    def from_side(step, sign):
+        spot = place(c_rank - sign * (step + 1), t_rank)
+        send, recv = (send_r, recv_r) if sign > 0 else (send_l, recv_l)
+        return remote(spot, spot, send.at[step], recv.at[step], sibling)
+
+    def sends(step, sign):
+        if sign > 0:
+            return jnp.logical_and(c_rank - step >= 0, c_rank < n - 1)
+        return jnp.logical_and(c_rank + step <= n - 1, c_rank > 0)
+
+    def receives(step, sign):
+        return c_rank - 1 - step >= 0 if sign > 0 else c_rank + 1 + step <= n - 1
+
+    def relay(index, t_index):
+        spot = place(index, t_index)
+        return remote(spot, spot, pair_send.at[index], pair_recv.at[index], sibling)
+
+    greet(n, ())
+    for sign in (1, -1):
+
+        @pl.when(sends(0, sign))
+        def _(sign=sign):
+            to_side(0, sign).start()
+
     own = place(c_rank, t_rank)
-    sends = [
-        remote(x_ref, own, send_sem.at[k], recv_sem.at[k], {"ctx": lax.rem(c_rank + k, n)})
-        for k in range(1, n)
-    ]
-    for send in sends:
-        send.start()
-    pair = [remote(x_ref, own, pair_send.at[0], pair_recv.at[0], sibling)]
-    pair[0].start()
+    own_pair = remote(x_ref, own, pair_send.at[c_rank], pair_recv.at[c_rank], sibling)
+    own_pair.start()
     keep = pltpu.make_async_copy(x_ref, own, own_sem)
     keep.start()
-    for k in range(1, n):
-        spot = place(lax.rem(c_rank + n - k, n), t_rank)
-        remote(x_ref, spot, send_sem.at[k], recv_sem.at[k], sibling).wait_recv()
-        relay = remote(spot, spot, pair_send.at[k], pair_recv.at[k], sibling)
-        relay.start()
-        pair.append(relay)
+    for step in range(n - 1):
+        for sign in (1, -1):
+
+            @pl.when(receives(step, sign))
+            def _(step=step, sign=sign):
+                from_side(step, sign).wait_recv()
+                if step + 1 < n - 1:
+
+                    @pl.when(sends(step + 1, sign))
+                    def _():
+                        to_side(step + 1, sign).start()
+
+                relay(c_rank - sign * (step + 1), t_rank).start()
+
     keep.wait()
-    for send in sends:
-        send.wait_send()
-    for k in range(n):
-        pair[k].wait_send()
-        spot = place(lax.rem(c_rank + n - k, n), 1 - t_rank)
-        remote(x_ref, spot, pair_send.at[k], pair_recv.at[k], sibling).wait_recv()
+    own_pair.wait_send()
+    relay(c_rank, 1 - t_rank).wait_recv()
+    for step in range(n - 1):
+        for sign in (1, -1):
+
+            @pl.when(sends(step, sign))
+            def _(step=step, sign=sign):
+                to_side(step, sign).wait_send()
+
+            @pl.when(receives(step, sign))
+            def _(step=step, sign=sign):
+                relay(c_rank - sign * (step + 1), t_rank).wait_send()
+                relay(c_rank - sign * (step + 1), 1 - t_rank).wait_recv()
 
 
 def gather_rows(own_half, n):
@@ -118,10 +174,7 @@
         in_specs=[pl.BlockSpec(memory_space=pl.ANY)],
         out_specs=pl.BlockSpec(memory_space=pl.ANY),
         scratch_shapes=[
-            pltpu.SemaphoreType.DMA((n,)),
-            pltpu.SemaphoreType.DMA((n,)),
-            pltpu.SemaphoreType.DMA((n,)),
-            pltpu.SemaphoreType.DMA((n,)),
+            *[pltpu.SemaphoreType.DMA((n,)) for _ in range(6)],
             pltpu.SemaphoreType.DMA,
         ],
         compiler_params=pltpu.CompilerParams(collective_id=0, has_side_effects=True),
@@ -129,104 +182,261 @@
     )(own_half)
 
 
-def scatter_kernel(
-    n,
-    share,
-    a_ref,
-    b_ref,
-    out_ref,
-    mine,
-    give,
-    take,
-    z_give,
-    z_take,
-    give_sem,
-    take_sem,
-    z_give_sem,
-    z_take_sem,
-    out_sems,
-):
-    c_rank = lax.axis_index("ctx")
+class LineScatter:
+    def __init__(self, n, a_ref, b_ref, scratch):
+        self.n, self.a_ref, self.b_ref = n, a_ref, b_ref
+        self.mine, self.give, self.take, self.z_give, self.z_take = scratch[:5]
+        self.give_sem, self.take_sem, self.z_give_sem, self.z_take_sem = scratch[5:9]
+        self.c_rank, self.t_rank = lax.axis_index("ctx"), lax.axis_index("tp")
+
+    def column_part(self, block, t_index):
+        half = self.mine.shape[2]
+        weight = self.b_ref[pl.ds(pl.multiple_of(t_index * half, half), half), :]
+        return matmul_right_t(block, weight)
+
+    def pair(self, j):
+        return remote(
+            self.give.at[j],
+            self.take.at[j],
+            self.give_sem.at[j],
+            self.take_sem.at[j],
+            {"tp": 1 - self.t_rank},
+        )
+
+    def onward(self, j, sign):
+        return remote(
+            self.z_give.at[j],
+            self.z_take.at[j],
+            self.z_give_sem.at[j],
+            self.z_take_sem.at[j],
+            {"ctx": self.c_rank + sign},
+        )
+
+    def onward_last(self, j):
+        return remote(
+            self.z_give.at[j],
+            self.z_take.at[self.n],
+            self.z_give_sem.at[j],
+            self.z_take_sem.at[self.n],
+            {"ctx": self.c_rank - 1},
+        )
+
+    def inward(self, slot):
+        return remote(
+            self.z_take.at[slot],
+            self.z_take.at[slot],
+            self.z_take_sem.at[slot],
+            self.z_take_sem.at[slot],
+            {"tp": 1 - self.t_rank},
+        )
+
+    def each(self, body):
+        for distance in range(self.n - 1, -1, -1):
+            for sign in (1, -1) if distance > 0 else (1,):
+                j = self.c_rank + sign * distance
+                inside = j < self.n if sign > 0 else j >= 0
+
+                @pl.when(inside)
+                def _(j=j, sign=sign, distance=distance):
+                    body(j, sign, distance)
+
+    def products(self, j, sign, distance):
+        rows = self.mine.shape[1]
+        block = self.a_ref[pl.ds(pl.multiple_of(j * rows, rows), rows), :]
+        self.give[j] = self.column_part(block, 1 - self.t_rank).astype(self.give.dtype)
+        self.pair(j).start()
+        self.mine[j] = self.column_part(block, self.t_rank)
+
+    def add_inward(self, j, slot):
+        self.inward(slot).wait_recv()
+        self.mine[j] += self.z_take[slot].astype(jnp.float32)
+
+    def passing(self, j, sign, distance):
+        self.pair(j).wait_recv()
+        self.mine[j] += self.take[j].astype(jnp.float32)
+        behind = self.c_rank > 0 if sign > 0 else self.c_rank < self.n - 1
+
+        @pl.when(behind)
+        def _():
+            self.add_inward(j, j)
+
+        if distance == 0:
+
+            @pl.when(self.c_rank < self.n - 1)
+            def _():
+                self.add_inward(j, self.n)
+
+            return
+        self.z_give[j] = self.mine[j].astype(self.z_give.dtype)
+        if sign < 0 and distance == 1:
+            self.onward_last(j).start()
+        else:
+            self.onward(j, sign).start()
+
+    def ending(self, j, sign, distance):
+        self.pair(j).wait_send()
+        if distance > 0:
+            self.onward(j, sign).wait_send()
+
+
+def scatter_kernel(n, parts, a_ref, b_ref, *rest):
+    fsdp_size = parts
+    if fsdp_size:
+        pack_ref, out_ref, taken_ref = rest[:3]
+        rest = rest[3:]
+        f_send, f_recv = rest[10:]
+    else:
+        out_ref, rest = rest[0], rest[1:]
+    out_sems = rest[9]
     t_rank = lax.axis_index("tp")
-    rows, half = mine.shape[1], mine.shape[2]
     sibling = {"tp": 1 - t_rank}
-    greet([{"ctx": lax.rem(c_rank + k, n)} for k in range(1, n)] + [sibling])
-    order = list(range(1, n)) + [0]
-
-    def column_part(block, t_index):
-        weight = b_ref[pl.ds(pl.multiple_of(t_index * half, half), half), :]
-        return matmul_right_t(block, weight)
-
-    pair = {}
-    for k in order:
-        target = lax.rem(c_rank + k, n)
-        block = a_ref[pl.ds(pl.multiple_of(target * rows, rows), rows), :]
-        give[k] = column_part(block, 1 - t_rank).astype(give.dtype)
-        pair[k] = remote(give.at[k], take.at[k], give_sem.at[k], take_sem.at[k], sibling)
-        pair[k].start()
-        mine[k] = column_part(block, t_rank)
-    sends = {}
-    for k in order:
-        pair[k].wait_recv()
-        if k > 0:
-            z_give[k] = (mine[k] + take[k].astype(jnp.float32)).astype(z_give.dtype)
-            sends[k] = remote(
-                z_give.at[k],
-                z_take.at[k],
-                z_give_sem.at[k],
-                z_take_sem.at[k],
-                {"ctx": lax.rem(c_rank + k, n)},
+    greet(n, (("fsdp", fsdp_size),) if fsdp_size else ())
+    moves = []
+    if fsdp_size:
+        f_rank = lax.axis_index("fsdp")
+        for k in range(1, fsdp_size):
+            peer = lax.rem(f_rank + k, fsdp_size)
+            moves.append(
+                remote(
+                    pack_ref.at[peer],
+                    taken_ref.at[k - 1],
+                    f_send.at[k],
+                    f_recv.at[k],
+                    {"fsdp": peer},
+                )
             )
-            sends[k].start()
-    total = mine[0] + take[0].astype(jnp.float32)
-    for k in range(1, n):
-        sends[k].wait_recv()
-        total = total + z_take[k].astype(jnp.float32)
-    if share:
-        out_ref[t_rank] = total
-        last = remote(
-            out_ref.at[t_rank], out_ref.at[t_rank], out_sems.at[0], out_sems.at[1], sibling
-        )
-        last.start()
-        last.wait_send()
-        remote(
-            out_ref.at[t_rank], out_ref.at[1 - t_rank], out_sems.at[0], out_sems.at[1], sibling
-        ).wait_recv()
-    else:
-        out_ref[0] = total
-    for k in order:
-        pair[k].wait_send()
-    for k in range(1, n):
-        sends[k].wait_send()
-
-
-def scatter_rows(left, right, n, share, kernel_id):
+            moves[-1].start()
+    line = LineScatter(n, a_ref, b_ref, rest)
+    line.each(line.products)
+    line.each(line.passing)
+    out_ref[t_rank] = line.mine[line.c_rank]
+    last = remote(out_ref.at[t_rank], out_ref.at[t_rank], out_sems.at[0], out_sems.at[1], sibling)
+    last.start()
+    last.wait_send()
+    remote(
+        out_ref.at[t_rank], out_ref.at[1 - t_rank], out_sems.at[0], out_sems.at[1], sibling
+    ).wait_recv()
+    line.each(line.ending)
+    for move in moves:
+        move.wait_recv()
+        move.wait_send()
+
+
+def line_scratch(n, rows, half):
+    sem = pltpu.SemaphoreType.DMA((n + 1,))
+    low = pltpu.VMEM((n, rows, half), jnp.bfloat16)
+    return [
+        pltpu.VMEM((n, rows, half), jnp.float32),
+        low,
+        low,
+        low,
+        pltpu.VMEM((n + 1, rows, half), jnp.bfloat16),
+        sem,
+        sem,
+        sem,
+        sem,
+    ]
+
+
+IN_VMEM = pl.BlockSpec(memory_space=pltpu.VMEM)
+ANYWHERE = pl.BlockSpec(memory_space=pl.ANY)
+
+
+def scatter_rows(left, right, n, kernel_id, pack=None):
     rows, half = left.shape[0] // n, right.shape[0] // 2
-    parts = 2 if share else 1
-    blocks = (n, rows, half)
-    sem = pltpu.SemaphoreType.DMA((n,))
+    out_shape = [jax.ShapeDtypeStruct((2, rows, half), jnp.float32)]
+    parts = 0
+    scratch = line_scratch(n, rows, half) + [pltpu.SemaphoreType.DMA((2,))]
+    if pack is not None:
+        parts = pack.shape[0]
+        out_shape.append(jax.ShapeDtypeStruct((parts - 1,) + pack.shape[1:], pack.dtype))
+        scratch += [pltpu.SemaphoreType.DMA((parts,)), pltpu.SemaphoreType.DMA((parts,))]
+    extra = () if pack is None else (pack,)
     return pl.pallas_call(
-        functools.partial(scatter_kernel, n, share),
-        out_shape=jax.ShapeDtypeStruct((parts, rows, half), jnp.float32),
-        in_specs=[pl.BlockSpec(memory_space=pltpu.VMEM)] * 2,
-        out_specs=pl.BlockSpec(memory_space=pltpu.VMEM),
-        scratch_shapes=[
-            pltpu.VMEM(blocks, jnp.float32),
-            pltpu.VMEM(blocks, jnp.bfloat16),
-            pltpu.VMEM(blocks, jnp.bfloat16),
-            pltpu.VMEM(blocks, jnp.bfloat16),
-            pltpu.VMEM(blocks, jnp.bfloat16),
-            sem,
-            sem,
-            sem,
-            sem,
-            pltpu.SemaphoreType.DMA((2,)),
-        ],
+        functools.partial(scatter_kernel, n, parts),
+        out_shape=out_shape,
+        in_specs=[IN_VMEM, IN_VMEM] + [ANYWHERE] * len(extra),
+        out_specs=[IN_VMEM] + [ANYWHERE] * len(extra),
+        scratch_shapes=scratch,
         compiler_params=pltpu.CompilerParams(
             collective_id=kernel_id, has_side_effects=True, vmem_limit_bytes=40 * 2**20
         ),
         name="scatter_rows",
-    )(left, right)
+    )(left, right, *extra)
+
+
+def finish_kernel(n, parts, a_ref, b_ref, pack_ref, small_ref, tok_ref, grads_ref, total_ref, *rest):
+    f_take, sf_take, sc_give, sc_take = rest[9:13]
+    f_send, f_recv, sf_send, sf_recv, g_send, g_recv, sc_send, sc_recv = rest[13:]
+    c_rank, f_rank = lax.axis_index("ctx"), lax.axis_index("fsdp")
+    greet(n, (("fsdp", parts), ("ctx", n)))
+    first, second = [], []
+    for k in range(1, parts):
+        peer = lax.rem(f_rank + k, parts)
+        at = {"fsdp": peer}
+        first.append(remote(pack_ref.at[peer], f_take.at[k], f_send.at[k], f_recv.at[k], at))
+        first.append(remote(small_ref, sf_take.at[k], sf_send.at[k], sf_recv.at[k], at))
+    for move in first:
+        move.start()
+    line = LineScatter(n, a_ref, b_ref, rest)
+    line.each(line.products)
+    total = pack_ref[f_rank].astype(jnp.float32)
+    small = small_ref[...]
+    for k in range(1, parts):
+        first[2 * k - 2].wait_recv()
+        first[2 * k - 1].wait_recv()
+        total = total + f_take[k].astype(jnp.float32)
+        small = small + sf_take[k]
+    grads_ref[c_rank] = total.astype(grads_ref.dtype)
+    sc_give[...] = small
+    for k in range(1, n):
+        peer = lax.rem(c_rank + k, n)
+        at = {"ctx": peer}
+        own = grads_ref.at[c_rank]
+        second.append(remote(own, own, g_send.at[k], g_recv.at[k], at))
+        second.append(remote(sc_give, sc_take.at[k], sc_send.at[k], sc_recv.at[k], at))
+    line.each(line.passing)
+    for move in second:
+        move.start()
+    tok_ref[...] = line.mine[c_rank]
+    for k in range(1, n):
+        spot = grads_ref.at[lax.rem(c_rank + n - k, n)]
+        remote(spot, spot, g_send.at[k], g_recv.at[k], {"ctx": lax.rem(c_rank + k, n)}).wait_recv()
+        second[2 * k - 1].wait_recv()
+        small = small + sc_take[k]
+    total_ref[...] = small
+    line.each(line.ending)
+    for move in first + second:
+        move.wait_send()
+
+
+def finish(left, right, pack, small, n, kernel_id):
+    rows, half = left.shape[0] // n, right.shape[0] // 2
+    parts = pack.shape[0]
+    f_sem, c_sem = pltpu.SemaphoreType.DMA((parts,)), pltpu.SemaphoreType.DMA((n,))
+    return pl.pallas_call(
+        functools.partial(finish_kernel, n, parts),
+        out_shape=[
+            jax.ShapeDtypeStruct((rows, half), jnp.float32),
+            jax.ShapeDtypeStruct((n,) + pack.shape[1:], pack.dtype),
+            jax.ShapeDtypeStruct(small.shape, jnp.float32),
+        ],
+        in_specs=[IN_VMEM] * 4,
+        out_specs=[IN_VMEM] * 3,
+        scratch_shapes=line_scratch(n, rows, half)
+        + [
+            pltpu.VMEM(pack.shape, pack.dtype),
+            pltpu.VMEM((parts,) + small.shape, jnp.float32),
+            pltpu.VMEM(small.shape, jnp.float32),
+            pltpu.VMEM((n,) + small.shape, jnp.float32),
+        ]
+        + [f_sem] * 4
+        + [c_sem] * 4,
+        compiler_params=pltpu.CompilerParams(
+            collective_id=kernel_id, has_side_effects=True, vmem_limit_bytes=40 * 2**20
+        ),
+        name="finish",
+    )(left, right, pack, small)
 
 
 def whole_rows(parts):
@@ -291,7 +501,7 @@
     mixed = jnp.einsum("hqk,khd->qhd", probs_low, head_v, preferred_element_type=jnp.float32)
     context = mixed.reshape(seq_slots, head_width).astype(jnp.bfloat16)
 
-    attended = whole_rows(scatter_rows(context, w_o, ctx_size, True, 1))
+    attended = whole_rows(scatter_rows(context, w_o, ctx_size, 1)[0])
     hidden_one, normed_one, inv_one = norm_forward(
         tok_float + attended + vec_rows[2], vec_rows[4], vec_rows[5]
     )
@@ -301,7 +511,7 @@
     pre_act = matmul_plain(hidden_seq, w_i) + unit_bias
     activated, gelu_pull = jax.vjp(gelu_exact, pre_act)
     act_low = activated.astype(jnp.bfloat16)
-    branch = whole_rows(scatter_rows(act_low, w_d, ctx_size, True, 2))
+    branch = whole_rows(scatter_rows(act_low, w_d, ctx_size, 2)[0])
     layer_out, normed_two, inv_two = norm_forward(
         hidden_one + branch + vec_rows[3], vec_rows[6], vec_rows[7]
     )
@@ -311,22 +521,26 @@
         own_columns(grad_two, tp_rank, half_width).astype(jnp.bfloat16), ctx_size
     )
     pre_low = gelu_pull(matmul_plain(branch_seq, w_d))[0].astype(jnp.bfloat16)
-    grad_hidden = grad_two + whole_rows(scatter_rows(pre_low, w_i, ctx_size, True, 3))
+    fsdp_rank = lax.axis_index("fsdp")
+    fsdp_size = lax.axis_size("fsdp")
+
+    def fsdp_blocks(*grads):
+        pack = jnp.concatenate([grad.astype(jnp.bfloat16) for grad in grads], axis=1)
+        return pack.reshape(fsdp_size, -1, pack.shape[1])
+
+    ffn_parts = fsdp_blocks(
+        matmul_left_t(hidden_seq, pre_low), matmul_left_t(branch_seq, act_low)
+    )
+    hidden_parts, ffn_taken = scatter_rows(pre_low, w_i, ctx_size, 3, ffn_parts)
+    ffn_own = (
+        lax.dynamic_index_in_dim(ffn_parts, fsdp_rank, 0, False).astype(jnp.float32)
+        + jnp.sum(ffn_taken.astype(jnp.float32), axis=0)
+    ).astype(jnp.bfloat16)
+    ffn_grads = lax.all_gather(ffn_own, "ctx", axis=0).astype(jnp.float32)
+    grad_hidden = grad_two + whole_rows(hidden_parts)
     grad_one = norm_backward(grad_hidden, vec_rows[4], normed_one, inv_one)
     attn_seq = gather_rows(
         own_columns(grad_one, tp_rank, half_width).astype(jnp.bfloat16), ctx_size
-    )
-
-    def share_gradient(pack):
-        own_rows = lax.psum_scatter(
-            pack.astype(jnp.bfloat16), "fsdp", scatter_dimension=0, tiled=True
-        )
-        return lax.all_gather(own_rows, "ctx", axis=0).astype(jnp.float32)
-
-    ffn_grads = share_gradient(
-        jnp.concatenate(
-            [matmul_left_t(hidden_seq, pre_low), matmul_left_t(branch_seq, act_low)], axis=1
-        )
     )
 
     grad_context = matmul_plain(attn_seq, w_o).astype(jnp.bfloat16)
@@ -345,15 +559,6 @@
         ],
         axis=1,
     )
-    attn_grads = share_gradient(
-        jnp.concatenate(
-            [matmul_left_t(tok_seq, qkv_low), matmul_left_t(attn_seq, context)], axis=1
-        )
-    )
-    grad_tokens = scatter_rows(qkv_low, w_qkv, ctx_size, False, 4)[0] + own_columns(
-        grad_one, tp_rank, half_width
-    )
-
     def spread(row, width):
         return lax.dynamic_update_slice_in_dim(
             jnp.zeros((width,), jnp.float32), row, ctx_rank * row.shape[0], 0
@@ -373,9 +578,13 @@
             spread(jnp.sum(pre_low.astype(jnp.float32), axis=0), unit_count * ctx_size),
         ]
     )
-    small_total = lax.psum(small_grads, ("fsdp", "ctx"))
-    fsdp_rank = lax.axis_index("fsdp")
-    fsdp_size = lax.axis_size("fsdp")
+    attn_parts = fsdp_blocks(matmul_left_t(tok_seq, qkv_low), matmul_left_t(attn_seq, context))
+    grad_rows, attn_grads, small_total = finish(
+        qkv_low, w_qkv, attn_parts, small_grads.reshape(-1, 128), ctx_size, 4
+    )
+    grad_tokens = grad_rows + own_columns(grad_one, tp_rank, half_width)
+    attn_grads = attn_grads.astype(jnp.float32)
+    small_total = small_total.reshape(-1)
     vector_grads = own_columns(
         small_total[: 8 * half_width].reshape(8, half_width), fsdp_rank, half_width // fsdp_size
     )

time: 508 us -> 388 us (0.76)
  waiting for transfers between devices: 61.7 us -> 0.07 us
  blocking collectives: 65.4 us -> 4.47 us
    reduce_scatter x2 -> x0, waiting for transfers between devices: 61.6 us -> none  [share_gradient(): lax.psum_scatter(pack.astype(jnp.bfloat16), 'fsdp', scatter_dimension=0,...]
    psum x1 -> x0, blocking collectives: 60.9 us -> none  [per_device(): small_total = lax.psum(small_grads, ('fsdp', 'ctx'))]
    pallas_call x4, Pallas kernels: 137 us -> 176 us  [the longest x3 93.9 us: scatter_rows(): pl.pallas_call(functools.partial(scatter_kernel, n, parts), out_shape=out...]
    pallas_call x4, Pallas kernels: 114 us -> 79.2 us  [gather_rows(): pl.pallas_call(functools.partial(gather_kernel, n), out_shape=jax.ShapeDt...]
    convert_element_type x2 -> x0, local copies, waits for them, and re-layouts: 6.99 us -> none  [share_gradient(): return lax.all_gather(own_rows, 'ctx', axis=0).astype(jnp.float32)]
    transpose x4 -> x2, local copies, waits for them, and re-layouts: 8.17 us -> 2.01 us  [stacked(): return blocks.transpose(0, 2, 1).reshape(-1, blocks.shape[1])]
    unnamed x66 -> x92, local copies, waits for them, and re-layouts: 10.5 us -> 16.3 us
  transfers between devices with their start and end apart: 6 -> 3, of which waited for: 2 -> 0; matrix products, arithmetic and copies ran while one was open for 8% -> 11% of each run, Pallas kernels for 26% -> 40%
where the time goes in v2:
time: 388 us; the launch traced here: 381 us
  Pallas kernels  255 us (66%)
  local copies, waits for them, and re-layouts  44.7 us (12%)
  matrix products  43.1 us (11%)
  other arithmetic  17.6 us (5%)
  between operations  15.7 us (4%)
  blocking collectives  4.47 us (1%)
    pallas_call x3, Pallas kernels, scatter_rows(): pl.pallas_call(functools.partial(scatter_kernel, n, parts), out_shape=out...  93.9 us
    pallas_call x1, Pallas kernels, finish(): pl.pallas_call(functools.partial(finish_kernel, n, parts), out_shape=[jax...  81.7 us
    pallas_call x4, Pallas kernels, gather_rows(): pl.pallas_call(functools.partial(gather_kernel, n), out_shape=jax.ShapeDt...  79.2 us
    unnamed x92, local copies, waits for them, and re-layouts  16.3 us
    dot_general x4, matrix products, matmul_plain(): return jnp.dot(left_side, right_side, preferred_element_type=jnp.float32)  13.5 us
    dot_general x4, matrix products, matmul_left_t(): lax.dot_general(left_side, right_side, (((0,), (0,)), ((), ())), preferre...  8.21 us
  transfers between devices with their start and end apart: 3, of which 0 were waited for; matrix products, arithmetic and copies ran while one was open for 11% of the time, Pallas kernels for 40%

profile of v2, /device:TPU:9, one launch (start us, length us, event | category | flops | bytes accessed | tf_op | source)
XLA Modules:
  0.0 380.6 jit_solution(7191727972400396516)
XLA Ops:
  13.0 2.2 all_gather.17
  16.8 2.3 all_gather.19
  19.1 20.4 %gather_rows.4 = bf16[1024,1024]{1,0:T(8,128)(2,1)} custom-call(bf16[256,512]{1,0:T(8,128)(2,1)} %x_ref.1), custom_call_target="tpu_custom_call" | custom-call | tf_op jit(solution)/shard_map/gather_rows/pallas_call | solution.py:171
  39.5 2.9 convolution_bitcast_fusion
  42.6 6.0 %fusion.57 = (f32[2,1024]{1,0:T(2,128)S(1)}, f32[2,1024,1024]{1,2,0:T(8,128)}) fusion(pred[1024]{0:T(1024)(128)(4,1)S(1)} %iota_compare_fusion, bf16[1024,2,64]{0,2,1:T(8,128)(2,1)S(1)} %bitcast.115, bf16[1024,2,64]{0,2,1:T(8,128)(2,1)S(1)} %bitcast.105), kind=kOutput, calls=%fused_computation.145 | convolution fusion | flops 274727936 | bytes 8922112 | tf_op jit(solution)/shard_map/sub | solution.py:498
  48.6 4.5 %fusion.17 = bf16[2,64,1024]{2,1,0:T(8,128)(2,1)S(1)} fusion(bf16[1024,2,64]{0,2,1:T(8,128)(2,1)S(1)} %bitcast.122, f32[2,1024,1024]{1,2,0:T(8,128)} %get-tuple-element.87, f32[2,1024]{1,0:T(2,128)S(1)} %get-tuple-element.86), kind=kOutput, calls=%fused_computation.39 | convolution fusion | flops 272760832 | bytes 8921088 | tf_op jit(solution)/shard_map/hqk,khd->qhd/dot_general | solution.py:501
  54.3 30.2 %scatter_rows.3 = f32[2,256,512]{2,1,0:T(8,128)S(1)} custom-call(bf16[1024,128]{1,0:T(8,128)(2,1)S(1)} %copy.57.a_ref, bf16[1024,128]{1,0:T(8,128)(2,1)S(1)} %slice.136.b_ref), custom_call_target="tpu_custom_call" | custom-call | tf_op jit(solution)/shard_map/scatter_rows/pallas_call | solution.py:355
  87.2 19.4 %gather_rows.5 = bf16[1024,1024]{1,0:T(8,128)(2,1)} custom-call(bf16[256,512]{1,0:T(8,128)(2,1)} %dynamic-slice_convert_fusion.1.x_ref), custom_call_target="tpu_custom_call" | custom-call | tf_op jit(solution)/shard_map/gather_rows/pallas_call | solution.py:171
  110.4 6.8 %multiply_convert_fusion.1 = (bf16[1024,512]{1,0:T(8,128)(2,1)S(1)}, f32[1024,512]{1,0:T(8,128)}, f32[1024,512]{1,0:T(8,128)}) fusion(f32[512]{0:T(512)S(1)} %dynamic-slice_convert_fusion.3, bf16[1024,1024]{1,0:T(8,128)(2,1)S(1)} %copy-done.20, bf16[1024,1024]{1,0:T(8,128)(2,1)S(1)} %copy-done.23), kind=kOutput, calls=%fused_computation.15 | convolution fusion | flops 1108344832 | bytes 8390656 | tf_op jit(solution)/shard_map/dot_general | solution.py:18
  117.2 30.9 %scatter_rows.4 = f32[2,256,512]{2,1,0:T(8,128)S(1)} custom-call(bf16[1024,512]{1,0:T(8,128)(2,1)S(1)} %get-tuple-element.58.a_ref, bf16[1024,512]{1,0:T(8,128)(2,1)S(1)} %get-tuple-element.69.b_ref), custom_call_target="tpu_custom_call" | custom-call | tf_op jit(solution)/shard_map/scatter_rows/pallas_call | solution.py:355
  152.0 20.0 %gather_rows.6 = bf16[1024,1024]{1,0:T(8,128)(2,1)} custom-call(bf16[256,512]{1,0:T(8,128)(2,1)} %dynamic-slice_convert_fusion.x_ref), custom_call_target="tpu_custom_call" | custom-call | tf_op jit(solution)/shard_map/gather_rows/pallas_call | solution.py:171
  172.0 3.0 convolution_convert_fusion
  176.1 2.0 convert_reduce_fusion.1
  181.9 2.9 copy.59
  186.0 32.8 %scatter_rows.5 = (f32[2,256,512]{2,1,0:T(8,128)S(1)}, bf16[3,256,1024]{2,1,0:T(8,128)(2,1)S(1)}) custom-call(bf16[1024,512]{1,0:T(8,128)(2,1)S(1)} %copy-done.7, bf16[1024,512]{1,0:T(8,128)(2,1)S(1)} %get-tuple-element.68.b_ref, bf16[4,256,1024]{2,1,0:T(8,128)(2,1)S(1)} %bitcast.98), custom_call_target="tpu_custom_call" | custom-call | tf_op jit(solution)/shard_map/scatter_rows/pallas_call | solution.py:355
  223.6 19.4 %gather_rows.7 = bf16[1024,1024]{1,0:T(8,128)(2,1)} custom-call(bf16[256,512]{1,0:T(8,128)(2,1)} %dynamic-slice_convert_fusion.2.x_ref), custom_call_target="tpu_custom_call" | custom-call | tf_op jit(solution)/shard_map/gather_rows/pallas_call | solution.py:171
  243.0 2.9 convolution_convert_fusion.3
  247.9 5.6 %fusion.20 = bf16[2,64,1024]{2,1,0:T(8,128)(2,1)} fusion(bf16[1024,2,64]{0,2,1:T(8,128)(2,1)S(1)} %bitcast.119, f32[2,1024,1024]{1,2,0:T(8,128)} %get-tuple-element.87, f32[2,1024]{1,0:T(2,128)S(1)} %get-tuple-element.86), kind=kOutput, calls=%fused_computation.40 | convolution fusion | flops 272760832 | bytes 8921088 | tf_op jit(solution)/shard_map/hqk,qhd->khd/dot_general | solution.py:553
  255.1 2.5 multiply_convert_fusion
  257.6 2.1 convolution_convert_fusion.4
  271.6 81.7 %finish.1 = (f32[256,512]{1,0:T(8,128)S(1)}, bf16[4,256,512]{2,1,0:T(8,128)(2,1)S(1)}, f32[48,128]{1,0:T(8,128)S(1)}) custom-call(bf16[1024,384]{1,0:T(8,128)(2,1)S(1)} %get-tuple-element.53.a_ref, bf16[1024,384]{1,0:T(8,128)(2,1)S(1)} %copy-done.2, bf16[4,256,512]{2,1,0:T(8,128)(2,1)S(1)} %bitcast.100, f32[48,128]{1,0:T(8,128)S(1)} %bitcast.101), custom_call_target="tpu_custom_call" | custom-call | tf_op jit(solution)/shard_map/finish/pallas_call | solution.py:417
  365.3 2.8 copy.71
  368.2 2.4 fusion.54
  370.6 3.0 copy.75
  (180 shorter events, 56.3 us)
Async XLA Ops:
  7.2 3.7 copy-start
  7.2 32.3 %all-gather.4.cloned.1.call-start = ((), (), s32[]{:S(2)}) async-start(), calls=%async_computation | async-start | bytes 1310720 | tf_op jit(solution)/shard_map/all_gather | solution.py:469
  9.1 3.8 %copy-start.34 = (bf16[8,512]{1,0:T(8,128)(2,1)S(1)}, bf16[8,512]{1,0:T(8,128)(2,1)}, u32[]{:S(2)}) copy-start(bf16[8,512]{1,0:T(8,128)(2,1)} %param.18) | copy-start | bytes 24580
  10.0 6.8 %copy-start.31 = (bf16[256,512]{1,0:T(8,128)(2,1)S(1)}, bf16[256,512]{1,0:T(8,128)(2,1)}, u32[]{:S(2)}) copy-start(bf16[256,512]{1,0:T(8,128)(2,1)} %param.21) | copy-start | bytes 786436
  10.8 96.7 %all-gather.6.cloned.1.call-start = ((), (), s32[]{:S(2)}) async-start(), calls=%async_computation.1 | async-start | bytes 2621440 | tf_op jit(solution)/shard_map/all_gather | solution.py:470
  12.9 352.4 %all-gather.8.cloned.1.call-start = ((), (), s32[]{:S(2)}) async-start(), calls=%async_computation.2 | async-start | bytes 2621440 | tf_op jit(solution)/shard_map/all_gather | solution.py:539
  42.5 6.0 %copy-start.28 = (bf16[1024,128]{0,1:T(8,128)(2,1)}, bf16[1024,128]{0,1:T(8,128)(2,1)S(1)}, u32[]{:S(2)}) copy-start(bf16[1024,128]{0,1:T(8,128)(2,1)S(1)} %get-tuple-element.70) | copy-start | bytes 786436
  42.5 6.0 %copy-start.32 = (bf16[1024,128]{0,1:T(8,128)(2,1)}, bf16[1024,128]{0,1:T(8,128)(2,1)S(1)}, u32[]{:S(2)}) copy-start(bf16[1024,128]{0,1:T(8,128)(2,1)S(1)} %get-tuple-element.71) | copy-start | bytes 786436
  53.1 31.5 %copy-start.26 = (bf16[2,64,1024]{2,1,0:T(8,128)(2,1)}, bf16[2,64,1024]{2,1,0:T(8,128)(2,1)S(1)}, u32[]{:S(2)}) copy-start(bf16[2,64,1024]{2,1,0:T(8,128)(2,1)S(1)} %fusion.17) | copy-start | bytes 786436
  85.9 62.2 %copy-start.8 = (f32[256,1024]{1,0:T(8,128)}, f32[256,1024]{1,0:T(8,128)S(1)}, u32[]{:S(2)}) copy-start(f32[256,1024]{1,0:T(8,128)S(1)} %get-tuple-element.61) | copy-start | bytes 3145732
  86.2 20.4 %copy-start.25 = (bf16[1024,512]{1,0:T(8,128)(2,1)S(1)}, bf16[1024,512]{1,0:T(8,128)(2,1)}, u32[]{:S(2)}) copy-start(bf16[1024,512]{1,0:T(8,128)(2,1)} %all-gather.4.cloned.1.call-done) | copy-start | bytes 3145732
  149.8 22.2 %copy-start.12 = (f32[256,1024]{1,0:T(8,128)}, f32[256,1024]{1,0:T(8,128)S(1)}, u32[]{:S(2)}) copy-start(f32[256,1024]{1,0:T(8,128)S(1)} %get-tuple-element.55) | copy-start | bytes 3145732
  172.0 3.1 copy-start.22
  172.0 3.1 copy-start.24
  172.0 3.5 copy-start.35
  172.0 4.1 %copy-start.36 = (f32[1024,512]{1,0:T(8,128)S(1)}, f32[1024,512]{1,0:T(8,128)}, u32[]{:S(2)}) copy-start(f32[1024,512]{1,0:T(8,128)} %get-tuple-element.88) | copy-start | bytes 6291460
  221.9 21.1 %copy-start.27 = (bf16[2,64,1024]{2,1,0:T(8,128)(2,1)S(1)}, bf16[2,64,1024]{2,1,0:T(8,128)(2,1)}, u32[]{:S(2)}) copy-start(bf16[2,64,1024]{2,1,0:T(8,128)(2,1)} %copy-done.26) | copy-start | bytes 786436
  245.9 7.6 %slice-start = ((s8[8388608]{0:T(1024)(128)(4,1)}), s8[4194304]{0:T(1024)(128)(4,1)S(1)}, s32[]{:S(2)}) async-start(s8[8388608]{0:T(1024)(128)(4,1)} %bitcast.102), calls=%async_computation.3 | async-start | bytes 8388608
  247.9 5.7 %slice-start.1 = ((s8[8388608]{0:T(1024)(128)(4,1)}), s8[4194304]{0:T(1024)(128)(4,1)S(1)}, s32[]{:S(2)}) async-start(s8[8388608]{0:T(1024)(128)(4,1)} %bitcast.102), calls=%async_computation.4 | async-start | bytes 8388608
  247.9 5.7 %copy-start.33 = (bf16[1024,128]{0,1:T(8,128)(2,1)S(1)}, bf16[1024,128]{0,1:T(8,128)(2,1)}, u32[]{:S(2)}) copy-start(bf16[1024,128]{0,1:T(8,128)(2,1)} %copy-done.32) | copy-start | bytes 786436
  262.5 4.5 %copy-start.11 = (bf16[1024,1024]{1,0:T(8,128)(2,1)S(1)}, bf16[1024,1024]{1,0:T(8,128)(2,1)}, u32[]{:S(2)}) copy-start(bf16[1024,1024]{1,0:T(8,128)(2,1)} %gather_rows.4) | copy-start | bytes 6291460
  268.1 3.5 copy-start.2
  359.0 4.7 %copy-start.13 = (f32[256,1024]{1,0:T(8,128)S(1)}, f32[256,1024]{1,0:T(8,128)}, u32[]{:S(2)}) copy-start(f32[256,1024]{1,0:T(8,128)} %copy-done.12) | copy-start | bytes 3145732
  359.2 5.3 %copy-start.18 = (f32[256,1024]{1,0:T(8,128)S(1)}, f32[256,1024]{1,0:T(8,128)}, u32[]{:S(2)}) copy-start(f32[256,1024]{1,0:T(8,128)} %copy-done.17) | copy-start | bytes 3145732
  (18 other events, 33.0 us)
Sparse Core Ops, SparseCore 0:
  10.9 27.7 all-gather.3
  41.2 35.3 all-gather.5
  262.7 62.6 all-gather.7
